TPU v7x, 512 devices: a whole 4x8x8 slice. The times are simulated.
512 devices in a mesh: tm: 256 (over z, y, x), seq: 2 (over core).
Axes of the slice: x: 4, y: 8, z: 8, core: 2. Of those that a mesh axis runs over, the one named last changes fastest.
Arguments:
- latents: float32 [256, 256, 64], P('tm', 'seq'), may hold values from -6 to 6
- timesteps: int32 [256], replicated, may hold values from 1 to 1024, as said below
- modulation: float32 [256, 5, 2048], P('tm'), may hold values from -4 to 4
- w_in: bfloat16 [64, 2048], replicated, may hold values from -0.25 to 0.25
- w_query: bfloat16 [2048, 2048], P(None, 'seq')
- w_key: bfloat16 [2048, 2048], P(None, 'seq')
- w_value: bfloat16 [2048, 2048], P(None, 'seq'), may hold values from -0.125 to 0.125
- w_attn_out: bfloat16 [2048, 2048], P('seq'), may hold values from -0.375 to 0.375
- w_final: bfloat16 [2048, 64], replicated, may hold values from -0.125 to 0.125
Outputs:
- next_latents: float32 [256, 256, 64], P('tm', 'seq')
Inputs may be any that keep to these rules, and one draw needn't show every extreme that they name: `timesteps`: strictly decreasing; the first is 1024.
All inputs are finite; a program needn't handle non-finite values.
Results may differ from a plain program's by a relative error of at most 0.015.
Values may be sent and summed in bfloat16 or wider, within the bound.
No kernel may reach another device: no remote copies, remote signals or barrier semaphores. Data moves between devices by JAX's collectives and lax.ppermute only.
A program may use at most 128 MiB of HBM per device.

v0:
```python
import jax
import jax.numpy as jnp
from jax import lax
from jax.sharding import PartitionSpec as P

HEAD_DIM = 128
TSCALE = 1024


norm_eps = 1e-06


def layer_norm(values):
    center = values - jnp.mean(values, axis=-1, keepdims=True)
    spread = jnp.mean(center * center, axis=-1, keepdims=True)
    return center * lax.rsqrt(spread + norm_eps)


def modulated(hidden, modulate):
    return (layer_norm(hidden) * (1.0 + modulate[1]) + modulate[0]).astype(jnp.bfloat16)


def project_three(normed, w_query, w_key, w_value):
    return jnp.stack(
        [
            jnp.dot(normed, w_query, preferred_element_type=jnp.float32),
            jnp.dot(normed, w_key, preferred_element_type=jnp.float32),
            jnp.dot(normed, w_value, preferred_element_type=jnp.float32),
        ]
    ).astype(jnp.bfloat16)


def attend_heads(queries, keys_all, values_all):
    token_count = queries.shape[0]
    local_heads = queries.shape[1] // HEAD_DIM
    block_rows = min(512, token_count)
    query_blocks = queries.reshape(token_count // block_rows, block_rows, local_heads, HEAD_DIM)
    keys_heads = keys_all.reshape(token_count, local_heads, HEAD_DIM)
    values_heads = values_all.reshape(token_count, local_heads, HEAD_DIM)

    def one_block(query_block):
        scores = jnp.einsum(
            "qhd,khd->hqk", query_block, keys_heads, preferred_element_type=jnp.float32
        ) * HEAD_DIM ** (-0.5)
        row_peak = jnp.max(scores, axis=-1, keepdims=True)
        weights = jnp.exp(scores - row_peak)
        weights = (weights / jnp.sum(weights, axis=-1, keepdims=True)).astype(jnp.bfloat16)
        return jnp.einsum(
            "hqk,khd->qhd", weights, values_heads, preferred_element_type=jnp.float32
        ).astype(jnp.bfloat16)

    blocks_out = lax.map(one_block, query_blocks)
    return blocks_out.reshape(token_count, local_heads * HEAD_DIM)


def on_device(latents, timesteps, modulation, w_in, w_query, w_key, w_value, w_attn_out, w_final):
    own_latent = latents[0]
    modulate = modulation[0]
    own_hidden = jnp.dot(own_latent.astype(jnp.bfloat16), w_in, preferred_element_type=jnp.float32)
    own_normed = modulated(own_hidden, modulate)
    projected = project_three(
        lax.all_gather(own_normed, "seq", axis=0, tiled=True), w_query, w_key, w_value
    )
    head_mixed = attend_heads(projected[0], projected[1], projected[2])
    attended = lax.psum_scatter(
        jnp.dot(head_mixed, w_attn_out, preferred_element_type=jnp.float32).astype(jnp.bfloat16),
        "seq",
        scatter_dimension=0,
        tiled=True,
    ).astype(jnp.float32)
    resid = own_hidden + modulate[2] * attended
    final = (layer_norm(resid) * (1.0 + modulate[4]) + modulate[3]).astype(jnp.bfloat16)
    drift_rows = jnp.dot(final, w_final, preferred_element_type=jnp.float32)
    step_index = lax.axis_index("tm")
    step_count = lax.axis_size("tm")
    time_values = timesteps.astype(jnp.float32)
    current = time_values[step_index]
    following = jnp.where(
        step_index + 1 < step_count, time_values[jnp.minimum(step_index + 1, step_count - 1)], 0.0
    )
    step_size = (following - current) / TSCALE
    step_term = step_size * drift_rows
    lined_term = step_term.reshape(-1, 128)
    everyone = lax.all_gather(
        lined_term[None].astype(jnp.bfloat16), "tm", axis=0, tiled=True
    ).astype(jnp.float32)
    chosen = (jnp.arange(everyone.shape[0], dtype=jnp.int32) <= step_index).astype(jnp.float32)
    summed = jnp.einsum(
        "s,srl->rl",
        chosen,
        everyone,
        precision=lax.Precision.HIGHEST,
        preferred_element_type=jnp.float32,
    )
    return summed.reshape(own_latent.shape)[None]


def solution(mesh):
    placed = (
        P("tm", "seq", None),
        P(),
        P("tm", None, None),
        P(),
        P(None, "seq"),
        P(None, "seq"),
        P(None, "seq"),
        P("seq", None),
        P(),
    )
    return jax.shard_map(
        on_device, mesh=mesh, in_specs=placed, out_specs=P("tm", "seq", None), check_vma=False
    )
```

profile of v0, /device:TPU:1, one launch (start us, length us, event | category | flops | bytes accessed | tf_op | source)
XLA Modules:
  0.0 210.7 jit_solution(926037970799323713)
XLA Ops:
  6.5 0.0 copy-start
  6.5 0.0 all-gather.3.cloned.1.call-start
  6.5 0.8 fusion.34
  7.4 0.2 copy-done
  7.6 1.2 fusion.36
  8.7 0.3 multiply_reduce_fusion.2
  9.0 1.1 add_convert_fusion.1
  10.1 0.0 all-gather.3.cloned.1.call-update
  10.1 0.0 reduce-scatter.2.cloned.1.call-start
  10.1 24.2 %all-gather.3.cloned.1.call-done = bf16[256,2048]{1,0:T(8,128)(2,1)} async-done(((bf16[128,2048]{1,0:T(8,128)(2,1)}), bf16[256,2048]{1,0:T(8,128)(2,1)}) %all-gather.3.cloned.1.call-update) | async-done | bytes 1048592 | tf_op jit(solution)/shard_map/all_gather | solution.py:62
  34.4 0.0 copy-start.4
  34.4 3.8 %convolution_convert_fusion.4 = bf16[256,1024]{1,0:T(8,128)(2,1)S(1)} fusion(bf16[256,2048]{1,0:T(8,128)(2,1)} %all-gather.3.cloned.1.call-done, bf16[2048,1024]{1,0:T(8,128)(2,1)} %param.15), kind=kOutput, calls=%fused_computation.11 | convolution fusion | flops 1074003968 | bytes 5767168 | tf_op jit(solution)/shard_map/dot_general | solution.py:28
  38.2 0.2 copy.29
  38.4 0.0 copy-done.4
  38.4 0.0 copy-start.2
  38.4 3.6 %fusion.5 = bf16[32,8,8,128]{3,2,1,0:T(8,128)(2,1)S(1)} fusion(bf16[256,2048]{1,0:T(8,128)(2,1)S(1)} %copy-done.4, bf16[2048,1024]{1,0:T(8,128)(2,1)} %param.14), kind=kOutput, calls=%fused_computation.13 | convolution fusion | flops 1074003968 | bytes 5767168 | tf_op jit(solution)/shard_map/dot_general | solution.py:27
  42.1 0.0 copy-done.2
  42.1 2.1 fusion.4
  44.2 3.2 %fusion.37 = (f32[8,256]{1,0:T(8,128)S(1)}, f32[8,256,256]{1,2,0:T(8,128)}) fusion(bf16[32,8,8,128]{3,2,1,0:T(8,128)(2,1)S(1)} %fusion.5, bf16[32,8,8,128]{3,2,1,0:T(8,128)(2,1)} %fusion.4), kind=kOutput, calls=%fused_computation.46 | convolution fusion | flops 135790848 | bytes 3153920 | tf_op jit(solution)/shard_map/while/body/eval_jaxpr/sub | solution.py:46
  47.4 0.0 copy-start.3
  47.4 2.1 convolution_convert_fusion.1
  49.5 0.0 copy-start.1
  49.5 0.7 copy-done.3
  50.2 0.0 copy-start.5
  50.2 2.3 %convolution_convert_fusion = bf16[256,2048]{1,0:T(8,128)(2,1)} fusion(bf16[256,1024]{0,1:T(8,128)(2,1)S(1)} %bitcast.65, bf16[1024,2048]{1,0:T(8,128)(2,1)S(1)} %copy-done.3), kind=kOutput, calls=%fused_computation.3 | convolution fusion | flops 1074266112 | bytes 5767168 | tf_op jit(solution)/shard_map/dot_general | solution.py:66
  52.4 0.0 reduce-scatter.2.cloned.1.call-update
  52.5 0.0 all-gather.5.cloned.1.call-start
  52.5 0.0 copy-done.1
  52.6 0.6 fusion.35
  54.4 16.2 %reduce-scatter.2.cloned.1.call-done = bf16[128,2048]{1,0:T(8,128)(2,1)} async-done(((bf16[256,2048]{1,0:T(8,128)(2,1)}), bf16[128,2048]{1,0:T(8,128)(2,1)}) %reduce-scatter.2.cloned.1.call-update) | async-done | bytes 524304 | tf_op jit(solution)/shard_map/reduce_scatter | solution.py:65
  70.6 1.3 fusion.17
  71.9 1.4 multiply_reduce_fusion.1
  73.3 0.0 copy-done.5
  73.3 1.5 fusion.6
  74.8 0.1 copy.24
  74.9 0.7 convert_element_type.60
  75.6 0.0 all-gather.5.cloned.1.call-update
  75.7 123.2 %all-gather.5.cloned.1.call-done = bf16[256,64,128]{2,1,0:T(8,128)(2,1)} async-done(((bf16[1,64,128]{2,1,0:T(8,128)(2,1)}), bf16[256,64,128]{2,1,0:T(8,128)(2,1)}) %all-gather.5.cloned.1.call-update) | async-done | bytes 4194320 | tf_op jit(solution)/shard_map/all_gather | solution.py:84
  198.9 4.5 %fusion.1 = f32[1,64,128]{2,0,1:T(1,128)S(1)} fusion(pred[256,1,1]{0,1,2:T(4,128)(4,1)S(1)} %reshape.73, bf16[256,64,128]{2,1,0:T(8,128)(2,1)} %all-gather.5.cloned.1.call-done), kind=kOutput, calls=%fused_computation.1 | convolution fusion | flops 4194304 | bytes 4227328 | tf_op jit(solution)/shard_map/s,srl->rl/dot_general | solution.py:88
  203.4 0.1 broadcast_in_dim_reshape.4
  203.5 0.7 copy.25
  (7 shorter events, 0.0 us)
Async XLA Ops:
  6.5 1.0 copy-start
  6.5 27.8 %all-gather.3.cloned.1.call-start = ((), (), s32[]{:S(2)}) async-start(), calls=%async_computation.1 | async-start | bytes 1572864 | tf_op jit(solution)/shard_map/all_gather | solution.py:62
  10.1 60.5 %reduce-scatter.2.cloned.1.call-start = ((), (), s32[]{:S(2)}) async-start(), calls=%async_computation.2 | async-start | bytes 1572864 | tf_op jit(solution)/shard_map/reduce_scatter | solution.py:65
  34.4 4.1 %copy-start.4 = (bf16[256,2048]{1,0:T(8,128)(2,1)S(1)}, bf16[256,2048]{1,0:T(8,128)(2,1)}, u32[]{:S(2)}) copy-start(bf16[256,2048]{1,0:T(8,128)(2,1)} %all-gather.3.cloned.1.call-done) | copy-start | bytes 3145732
  38.4 3.6 %copy-start.2 = (bf16[2048,1024]{1,0:T(8,128)(2,1)S(1)}, bf16[2048,1024]{1,0:T(8,128)(2,1)}, u32[]{:S(2)}) copy-start(bf16[2048,1024]{1,0:T(8,128)(2,1)} %param.13) | copy-start | bytes 12582916
  47.4 2.8 %copy-start.3 = (bf16[1024,2048]{1,0:T(8,128)(2,1)S(1)}, bf16[1024,2048]{1,0:T(8,128)(2,1)}, u32[]{:S(2)}) copy-start(bf16[1024,2048]{1,0:T(8,128)(2,1)} %param.16) | copy-start | bytes 12582916
  49.5 3.1 %copy-start.1 = (s32[256]{0:T(256)S(1)}, s32[256]{0:T(256)}, u32[]{:S(2)}) copy-start(s32[256]{0:T(256)} %param.10) | copy-start | bytes 3076
  50.2 23.1 %copy-start.5 = (bf16[2048,64]{0,1:T(8,128)(2,1)S(1)}, bf16[2048,64]{0,1:T(8,128)(2,1)}, u32[]{:S(2)}) copy-start(bf16[2048,64]{0,1:T(8,128)(2,1)} %param.17) | copy-start | bytes 786436
  52.5 146.4 %all-gather.5.cloned.1.call-start = ((), (), s32[]{:S(2)}) async-start(), calls=%async_computation.3 | async-start | bytes 4210688 | tf_op jit(solution)/shard_map/all_gather | solution.py:84
Sparse Core Ops, SparseCore 0:
  10.2 24.1 all-gather.2
  52.6 17.9 reduce-scatter.1
  75.8 123.0 all-gather.4
where the time goes:
time: 214 us; the launch traced here: 211 us
  waiting for transfers between devices  164 us (77%)
  matrix products  24.2 us (11%)
  between operations  14.5 us (7%)
  other arithmetic  4.84 us (2%)
  local copies, waits for them, and re-layouts  3.37 us (2%)
    all_gather x1, waiting for transfers between devices, on_device(): lax.all_gather(lined_term[None].astype(jnp.bfloat16), 'tm', axis=0, tiled...  123 us
    all_gather x1, waiting for transfers between devices, on_device(): lax.all_gather(own_normed, 'seq', axis=0, tiled=True)  24.2 us
    reduce_scatter x1, waiting for transfers between devices, on_device(): lax.psum_scatter(jnp.dot(head_mixed, w_attn_out, preferred_element_type=j...  16.2 us
    dot_general x1, matrix products, on_device(): jnp.einsum('s,srl->rl', chosen, everyone, precision=lax.Precision.HIGHEST...  4.48 us
  transfers between devices with their start and end apart: 3, of which 3 were waited for; matrix products, arithmetic and copies ran while one was open for 0% of the time, Pallas kernels for 0%

commit v1 on v0

v1 whole, which is shorter than its diff:
```python
import jax
import jax.numpy as jnp
from jax import lax
from jax.sharding import PartitionSpec as P

HEAD_DIM = 128
TSCALE = 1024
STAGES = (4, 8, 8)

norm_eps = 1e-06


def layer_norm(values):
    center = values - jnp.mean(values, axis=-1, keepdims=True)
    spread = jnp.mean(center * center, axis=-1, keepdims=True)
    return center * lax.rsqrt(spread + norm_eps)


def modulated(hidden, modulate):
    return (layer_norm(hidden) * (1.0 + modulate[1]) + modulate[0]).astype(jnp.bfloat16)


def attend_heads(queries, keys_all, values_all):
    token_count = queries.shape[0]
    local_heads = queries.shape[1] // HEAD_DIM
    queries = queries.reshape(token_count, local_heads, HEAD_DIM)
    keys_heads = keys_all.reshape(token_count, local_heads, HEAD_DIM)
    values_heads = values_all.reshape(token_count, local_heads, HEAD_DIM)
    scores = jnp.einsum(
        "qhd,khd->hqk", queries, keys_heads, preferred_element_type=jnp.float32
    ) * HEAD_DIM ** (-0.5)
    row_peak = jnp.max(scores, axis=-1, keepdims=True)
    weights = jnp.exp(scores - row_peak)
    weights = (weights / jnp.sum(weights, axis=-1, keepdims=True)).astype(jnp.bfloat16)
    mixed = jnp.einsum(
        "hqk,khd->qhd", weights, values_heads, preferred_element_type=jnp.float32
    ).astype(jnp.bfloat16)
    return mixed.reshape(token_count, local_heads * HEAD_DIM)


def along(stage, count):
    below = 1
    for size in STAGES[:stage]:
        below *= size
    size = STAGES[stage]
    return [
        [outer * below * size + place * below + inner for place in range(size)]
        for outer in range(count // (below * size))
        for inner in range(below)
    ]


def prefix_over_steps(term):
    count = lax.axis_size("tm")
    place = lax.axis_index("tm")
    prefix = term
    total = term
    for stage, size in enumerate(STAGES):
        here = place % size
        place = place // size
        block = jnp.broadcast_to(total.astype(jnp.bfloat16)[None], (size,) + total.shape)
        parts = lax.all_to_all(
            block, "tm", 0, 0, axis_index_groups=along(stage, count)
        ).astype(jnp.float32)
        earlier = (jnp.arange(size, dtype=jnp.int32) < here)[:, None, None]
        prefix = prefix + jnp.sum(jnp.where(earlier, parts, 0.0), axis=0)
        total = jnp.sum(parts, axis=0)
    return prefix


def on_device(latents, timesteps, modulation, w_in, w_query, w_key, w_value, w_attn_out, w_final):
    swap = [(0, 1), (1, 0)]
    own_latent = latents[0].T
    other_latent = lax.ppermute(own_latent, "seq", swap)
    modulate = modulation[0]

    def hidden_of(latent):
        return lax.dot_general(
            latent.astype(jnp.bfloat16), w_in, (((0,), (0,)), ((), ())), preferred_element_type=jnp.float32
        )

    own_hidden = hidden_of(own_latent)
    normed = jnp.concatenate(
        [modulated(own_hidden, modulate), modulated(hidden_of(other_latent), modulate)]
    )

    def project(weight):
        return jnp.dot(normed, weight, preferred_element_type=jnp.float32).astype(jnp.bfloat16)

    head_mixed = attend_heads(project(w_query), project(w_key), project(w_value))
    partial = jnp.dot(head_mixed, w_attn_out, preferred_element_type=jnp.float32).astype(jnp.bfloat16)
    token_count = own_hidden.shape[0]
    received = lax.ppermute(partial[token_count:], "seq", swap)
    attended = partial[:token_count].astype(jnp.float32) + received.astype(jnp.float32)
    resid = own_hidden + modulate[2] * attended
    final = (layer_norm(resid) * (1.0 + modulate[4]) + modulate[3]).astype(jnp.bfloat16)
    drift = lax.dot_general(
        w_final, final, (((0,), (1,)), ((), ())), preferred_element_type=jnp.float32
    )
    step_index = lax.axis_index("tm")
    step_count = lax.axis_size("tm")
    time_values = timesteps.astype(jnp.float32)
    current = time_values[step_index]
    following = jnp.where(
        step_index + 1 < step_count, time_values[jnp.minimum(step_index + 1, step_count - 1)], 0.0
    )
    step_size = (following - current) / TSCALE
    return prefix_over_steps(step_size * drift).T[None]


def solution(mesh):
    placed = (
        P("tm", "seq", None),
        P(),
        P("tm", None, None),
        P(),
        P(None, "seq"),
        P(None, "seq"),
        P(None, "seq"),
        P("seq", None),
        P(),
    )
    return jax.shard_map(
        on_device, mesh=mesh, in_specs=placed, out_specs=P("tm", "seq", None), check_vma=False
    )
```

time: 214 us -> 75.9 us (0.35)
  the two profiles are of different devices: /device:TPU:1 before, /device:TPU:2 now
where the time goes in v1:
time: 75.9 us; the launch traced here: 75.2 us
  starting transfers between devices  26.6 us (35%)
  waiting for transfers between devices  22 us (29%)
  matrix products  15.4 us (20%)
  local copies, waits for them, and re-layouts  5.42 us (7%)
  other arithmetic  4.13 us (5%)
  between operations  1.62 us (2%)
    all_to_all x3, starting transfers between devices, prefix_over_steps(): lax.all_to_all(block, 'tm', 0, 0, axis_index_groups=along(stage, count))  22.3 us
    all_to_all x3, waiting for transfers between devices, prefix_over_steps(): lax.all_to_all(block, 'tm', 0, 0, axis_index_groups=along(stage, count))  22 us
    dot_general x3, matrix products, project(): jnp.dot(normed, weight, preferred_element_type=jnp.float32)  6.96 us
    sub x1, matrix products, attend_heads(): weights = jnp.exp(scores - row_peak)  3.18 us
    unnamed x12, local copies, waits for them, and re-layouts  2.56 us
    ppermute x1, starting transfers between devices, on_device(): received = lax.ppermute(partial[token_count:], 'seq', swap)  2.4 us
    dot_general x1, matrix products, attend_heads(): jnp.einsum('hqk,khd->qhd', weights, values_heads, preferred_element_type=...  2.06 us
    broadcast_in_dim x3, local copies, waits for them, and re-layouts, prefix_over_steps(): jnp.broadcast_to(total.astype(jnp.bfloat16)[None], (size,) + total.shape)  1.94 us
  transfers between devices with their start and end apart: 5, of which 3 were waited for; matrix products, arithmetic and copies ran while one was open for 4% of the time, Pallas kernels for 0%

profile of v1, /device:TPU:2, one launch (start us, length us, event | category | flops | bytes accessed | tf_op | source)
XLA Modules:
  0.0 75.2 jit_solution(2350416534087812640)
XLA Ops:
  0.0 0.0 copy-start
  0.0 0.8 %bitcast_convert_fusion = bf16[64,128]{1,0:T(8,128)(2,1)S(1)} fusion(f32[1,128,64]{1,2,0:T(8,128)} %param.9), kind=kLoop, calls=%fused_computation.65 | loop fusion | flops 8192 | bytes 49152
  0.8 1.9 %collective-permute-start = (bf16[64,128]{1,0:T(8,128)(2,1)S(1)}, bf16[64,128]{1,0:T(8,128)(2,1)S(1)}, u32[]{:S(2)}, u32[]{:S(2)}) collective-permute-start(bf16[64,128]{1,0:T(8,128)(2,1)S(1)} %bitcast_convert_fusion), channel_id=1, source_target_pairs={{0,1},{1,0},{2,3},{3,2},{4,5},{5,4},{6,7},{7,6},{8,9},{9,8},{10,11... | collective-permute-start | bytes 49160 | tf_op jit(solution)/shard_map/ppermute | solution.py:74
  2.7 0.0 copy-done
  2.7 1.2 %fusion.39 = (f32[128]{0:T(128)S(1)}, f32[128,2048]{1,0:T(8,128)S(1)}) fusion(bf16[64,2048]{1,0:T(8,128)(2,1)S(1)} %copy-done, f32[1,128,64]{1,2,0:T(8,128)} %param.9), kind=kOutput, calls=%fused_computation.61 | convolution fusion | flops 33816448 | bytes 1344000 | tf_op jit(solution)/shard_map/dot_general | solution.py:78
  3.9 0.8 %slice_add_fusion = (f32[1,1,2048]{2,0,1:T(1,128)S(1)}, f32[1,1,2048]{2,0,1:T(1,128)S(1)}, f32[1,1,2048]{2,0,1:T(1,128)S(1)}, f32[1,1,2048]{2,0,1:T(1,128)S(1)}, f32[1,1,2048]{2,0,1:T(1,128)S(1)}) fusion(f32[1,5,2048]{2,0,1:T(1,128)} %param.11), kind=kLoop, calls=%fused_computation.43 | loop fusion | flops 4096 | bytes 81920 | tf_op jit(solution)/shard_map/add | solution.py:96
  4.7 0.3 multiply_reduce_fusion.3
  5.0 0.0 collective-permute-done
  5.0 0.4 fusion.40
  5.4 0.0 copy-start.2
  5.4 0.3 multiply_reduce_fusion.2
  5.7 0.5 add_convert_fusion.2
  6.1 1.4 %copy-done.2 = bf16[2048,1024]{1,0:T(8,128)(2,1)S(1)} copy-done((bf16[2048,1024]{1,0:T(8,128)(2,1)S(1)}, bf16[2048,1024]{1,0:T(8,128)(2,1)}, u32[]{:S(2)}) %copy-start.2) | copy-done | bytes 4194328
  7.6 1.3 %convolution_convert_fusion.4 = bf16[256,1024]{1,0:T(8,128)(2,1)S(1)} fusion(bf16[2048,1024]{1,0:T(8,128)(2,1)S(1)} %copy-done.2, bf16[128,2048]{1,0:T(8,128)(2,1)S(1)} %get-tuple-element.13, bf16[128,2048]{1,0:T(8,128)(2,1)S(1)} %get-tuple-element.12), kind=kOutput, calls=%fused_computation.9 | convolution fusion | flops 1076101120 | bytes 5767168 | tf_op jit(solution)/shard_map/dot_general | solution.py:88
  8.9 0.2 copy.19
  9.1 0.0 copy-start.3
  9.1 3.6 %fusion.3 = bf16[32,8,8,128]{3,2,1,0:T(8,128)(2,1)S(1)} fusion(bf16[2048,1024]{1,0:T(8,128)(2,1)} %param.14, bf16[128,2048]{1,0:T(8,128)(2,1)S(1)} %get-tuple-element.13, bf16[128,2048]{1,0:T(8,128)(2,1)S(1)} %get-tuple-element.12), kind=kOutput, calls=%fused_computation.11 | convolution fusion | flops 1076101120 | bytes 5767168 | tf_op jit(solution)/shard_map/dot_general | solution.py:88
  12.7 0.0 copy-done.3
  12.7 2.1 %fusion.2 = bf16[32,8,8,128]{3,2,1,0:T(8,128)(2,1)} fusion(bf16[2048,1024]{1,0:T(8,128)(2,1)S(1)} %copy-done.3, bf16[128,2048]{1,0:T(8,128)(2,1)S(1)} %get-tuple-element.13, bf16[128,2048]{1,0:T(8,128)(2,1)S(1)} %get-tuple-element.12), kind=kOutput, calls=%fused_computation.10 | convolution fusion | flops 1076101120 | bytes 5767168 | tf_op jit(solution)/shard_map/dot_general | solution.py:88
  14.8 3.2 %fusion.41 = (f32[8,256]{1,0:T(8,128)S(1)}, f32[8,256,256]{1,2,0:T(8,128)}) fusion(bf16[32,8,8,128]{3,2,1,0:T(8,128)(2,1)S(1)} %fusion.3, bf16[32,8,8,128]{3,2,1,0:T(8,128)(2,1)} %fusion.2), kind=kOutput, calls=%fused_computation.63 | convolution fusion | flops 135790848 | bytes 3153920 | tf_op jit(solution)/shard_map/sub | solution.py:33
  18.0 0.0 copy-start.4
  18.0 2.1 %convolution_convert_fusion.1 = bf16[8,128,256]{2,1,0:T(8,128)(2,1)S(1)} fusion(bf16[256,8,128]{0,2,1:T(8,128)(2,1)S(1)} %bitcast.80, f32[8,256,256]{1,2,0:T(8,128)} %get-tuple-element.21, f32[8,256]{1,0:T(8,128)S(1)} %get-tuple-element.20), kind=kOutput, calls=%fused_computation.6 | convolution fusion | flops 135528448 | bytes 3153920 | tf_op jit(solution)/shard_map/hqk,khd->qhd/dot_general | solution.py:35
  20.0 0.7 copy-done.4
  20.8 0.0 copy-start.1
  20.8 1.3 %convolution_convert_fusion = bf16[256,2048]{1,0:T(8,128)(2,1)S(1)} fusion(bf16[256,1024]{0,1:T(8,128)(2,1)S(1)} %bitcast.86, bf16[1024,2048]{1,0:T(8,128)(2,1)S(1)} %copy-done.4), kind=kOutput, calls=%fused_computation.1 | convolution fusion | flops 1074266112 | bytes 5767168 | tf_op jit(solution)/shard_map/dot_general | solution.py:91
  22.1 2.4 %collective-permute-start.1 = (bf16[128,2048]{1,0:T(8,128)(2,1)S(1)}, bf16[128,2048]{1,0:T(8,128)(2,1)S(1)}, u32[]{:S(2)}, u32[]{:S(2)}) collective-permute-start(bf16[128,2048]{1,0:T(8,128)(2,1)S(1)} %slice.36), channel_id=1, source_target_pairs={{0,1},{1,0},{2,3},{3,2},{4,5},{5,4},{6,7},{7,6},{8,9},{9,8},{10,11... | collective-permute-start | bytes 1572872 | tf_op jit(solution)/shard_map/ppermute | solution.py:93
  24.5 0.0 copy-done.1
  24.5 0.7 fusion.38
  26.6 0.0 collective-permute-done.1
  26.6 0.0 copy-start.5
  26.6 0.3 fusion.37
  26.9 0.3 multiply_reduce_fusion.1
  27.2 0.3 copy-done.5
  27.5 0.4 convolution_multiply_fusion
  27.9 0.6 broadcast_in_dim.39
  28.6 9.2 %all-to-all-start = ((bf16[4,64,128]{2,1,0:T(8,128)(2,1)}), bf16[4,64,128]{2,1,0:T(8,128)(2,1)S(1)}, u32[]{:S(2)}, u32[]{:S(2)}) async-start(bf16[4,64,128]{2,1,0:T(8,128)(2,1)} %broadcast_in_dim.39), calls=%async_computation | async-start | bytes 131072 | tf_op jit(solution)/shard_map/all_to_all | solution.py:62
  37.7 4.2 %all-to-all-done = bf16[4,64,128]{2,1,0:T(8,128)(2,1)S(1)} async-done(((bf16[4,64,128]{2,1,0:T(8,128)(2,1)}), bf16[4,64,128]{2,1,0:T(8,128)(2,1)S(1)}, u32[]{:S(2)}, u32[]{:S(2)}) %all-to-all-start) | async-done | bytes 65568 | tf_op jit(solution)/shard_map/all_to_all | solution.py:62
  41.9 0.7 broadcast_in_dim.42
  42.6 3.4 %all-to-all-start.1 = ((bf16[8,64,128]{2,1,0:T(8,128)(2,1)}), bf16[8,64,128]{2,1,0:T(8,128)(2,1)S(1)}, u32[]{:S(2)}, u32[]{:S(2)}) async-start(bf16[8,64,128]{2,1,0:T(8,128)(2,1)} %broadcast_in_dim.42), calls=%async_computation.1 | async-start | bytes 262144 | tf_op jit(solution)/shard_map/all_to_all | solution.py:62
  46.0 8.9 %all-to-all-done.1 = bf16[8,64,128]{2,1,0:T(8,128)(2,1)S(1)} async-done(((bf16[8,64,128]{2,1,0:T(8,128)(2,1)}), bf16[8,64,128]{2,1,0:T(8,128)(2,1)S(1)}, u32[]{:S(2)}, u32[]{:S(2)}) %all-to-all-start.1) | async-done | bytes 131104 | tf_op jit(solution)/shard_map/all_to_all | solution.py:62
  55.0 0.7 broadcast_in_dim.72
  55.6 9.8 %all-to-all-start.2 = ((bf16[8,64,128]{2,1,0:T(8,128)(2,1)}), bf16[8,64,128]{2,1,0:T(8,128)(2,1)S(1)}, u32[]{:S(2)}, u32[]{:S(2)}) async-start(bf16[8,64,128]{2,1,0:T(8,128)(2,1)} %broadcast_in_dim.72), calls=%async_computation.2 | async-start | bytes 262144 | tf_op jit(solution)/shard_map/all_to_all | solution.py:62
  65.4 0.1 select_reduce_fusion.2
  65.5 0.1 select_reduce_fusion.1
  65.6 8.9 %all-to-all-done.2 = bf16[8,64,128]{2,1,0:T(8,128)(2,1)S(1)} async-done(((bf16[8,64,128]{2,1,0:T(8,128)(2,1)}), bf16[8,64,128]{2,1,0:T(8,128)(2,1)S(1)}, u32[]{:S(2)}, u32[]{:S(2)}) %all-to-all-start.2) | async-done | bytes 131104 | tf_op jit(solution)/shard_map/all_to_all | solution.py:62
  74.5 0.1 select_reduce_fusion
  74.6 0.6 fusion.22
  (14 shorter events, 0.1 us)
Async XLA Ops:
  0.0 2.7 %copy-start = (bf16[64,2048]{1,0:T(8,128)(2,1)S(1)}, bf16[64,2048]{1,0:T(8,128)(2,1)}, u32[]{:S(2)}) copy-start(bf16[64,2048]{1,0:T(8,128)(2,1)} %param.12) | copy-start | bytes 786436
  0.8 4.2 %collective-permute-start = (bf16[64,128]{1,0:T(8,128)(2,1)S(1)}, bf16[64,128]{1,0:T(8,128)(2,1)S(1)}, u32[]{:S(2)}, u32[]{:S(2)}) collective-permute-start(bf16[64,128]{1,0:T(8,128)(2,1)S(1)} %bitcast_convert_fusion), channel_id=1, source_target_pairs={{0,1},{1,0},{2,3},{3,2},{4,5},{5,4},{6,7},{7,6},{8,9},{9,8},{10,11... | collective-permute-start | bytes 49160 | tf_op jit(solution)/shard_map/ppermute | solution.py:74
  5.4 2.2 %copy-start.2 = (bf16[2048,1024]{1,0:T(8,128)(2,1)S(1)}, bf16[2048,1024]{1,0:T(8,128)(2,1)}, u32[]{:S(2)}) copy-start(bf16[2048,1024]{1,0:T(8,128)(2,1)} %param.15) | copy-start | bytes 12582916
  9.1 3.6 %copy-start.3 = (bf16[2048,1024]{1,0:T(8,128)(2,1)S(1)}, bf16[2048,1024]{1,0:T(8,128)(2,1)}, u32[]{:S(2)}) copy-start(bf16[2048,1024]{1,0:T(8,128)(2,1)} %param.13) | copy-start | bytes 12582916
  18.0 2.8 %copy-start.4 = (bf16[1024,2048]{1,0:T(8,128)(2,1)S(1)}, bf16[1024,2048]{1,0:T(8,128)(2,1)}, u32[]{:S(2)}) copy-start(bf16[1024,2048]{1,0:T(8,128)(2,1)} %param.16) | copy-start | bytes 12582916
  20.8 3.7 %copy-start.1 = (s32[256]{0:T(256)S(1)}, s32[256]{0:T(256)}, u32[]{:S(2)}) copy-start(s32[256]{0:T(256)} %param.10) | copy-start | bytes 3076
  22.1 4.5 %collective-permute-start.1 = (bf16[128,2048]{1,0:T(8,128)(2,1)S(1)}, bf16[128,2048]{1,0:T(8,128)(2,1)S(1)}, u32[]{:S(2)}, u32[]{:S(2)}) collective-permute-start(bf16[128,2048]{1,0:T(8,128)(2,1)S(1)} %slice.36), channel_id=1, source_target_pairs={{0,1},{1,0},{2,3},{3,2},{4,5},{5,4},{6,7},{7,6},{8,9},{9,8},{10,11... | collective-permute-start | bytes 1572872 | tf_op jit(solution)/shard_map/ppermute | solution.py:93
  26.6 1.0 %copy-start.5 = (bf16[2048,64]{0,1:T(8,128)(2,1)S(1)}, bf16[2048,64]{0,1:T(8,128)(2,1)}, u32[]{:S(2)}) copy-start(bf16[2048,64]{0,1:T(8,128)(2,1)} %param.17) | copy-start | bytes 786436
  28.6 13.3 %all-to-all-start = ((bf16[4,64,128]{2,1,0:T(8,128)(2,1)}), bf16[4,64,128]{2,1,0:T(8,128)(2,1)S(1)}, u32[]{:S(2)}, u32[]{:S(2)}) async-start(bf16[4,64,128]{2,1,0:T(8,128)(2,1)} %broadcast_in_dim.39), calls=%async_computation | async-start | bytes 131072 | tf_op jit(solution)/shard_map/all_to_all | solution.py:62
  42.6 12.4 %all-to-all-start.1 = ((bf16[8,64,128]{2,1,0:T(8,128)(2,1)}), bf16[8,64,128]{2,1,0:T(8,128)(2,1)S(1)}, u32[]{:S(2)}, u32[]{:S(2)}) async-start(bf16[8,64,128]{2,1,0:T(8,128)(2,1)} %broadcast_in_dim.42), calls=%async_computation.1 | async-start | bytes 262144 | tf_op jit(solution)/shard_map/all_to_all | solution.py:62
  55.6 18.9 %all-to-all-start.2 = ((bf16[8,64,128]{2,1,0:T(8,128)(2,1)}), bf16[8,64,128]{2,1,0:T(8,128)(2,1)S(1)}, u32[]{:S(2)}, u32[]{:S(2)}) async-start(bf16[8,64,128]{2,1,0:T(8,128)(2,1)} %broadcast_in_dim.72), calls=%async_computation.2 | async-start | bytes 262144 | tf_op jit(solution)/shard_map/all_to_all | solution.py:62

commit v2 on v1

--- a/solution.py
+++ b/solution.py
@@ -5,7 +5,7 @@
 
 HEAD_DIM = 128
 TSCALE = 1024
-STAGES = (4, 8, 8)
+NX, NY, NZ = 4, 8, 8
 
 norm_eps = 1e-06
 
@@ -38,34 +38,41 @@
     return mixed.reshape(token_count, local_heads * HEAD_DIM)
 
 
-def along(stage, count):
-    below = 1
-    for size in STAGES[:stage]:
-        below *= size
-    size = STAGES[stage]
-    return [
-        [outer * below * size + place * below + inner for place in range(size)]
-        for outer in range(count // (below * size))
-        for inner in range(below)
-    ]
+def same(count, key):
+    groups = {}
+    for step in range(count):
+        groups.setdefault(key(*place_of(step)), []).append(step)
+    return list(groups.values())
+
+
+def place_of(step):
+    return step % NX, step // NX % NY, step // (NX * NY)
+
+
+def step_of(x, y, z):
+    return (z * NY + y) * NX + x
 
 
 def prefix_over_steps(term):
     count = lax.axis_size("tm")
-    place = lax.axis_index("tm")
-    prefix = term
-    total = term
-    for stage, size in enumerate(STAGES):
-        here = place % size
-        place = place // size
-        block = jnp.broadcast_to(total.astype(jnp.bfloat16)[None], (size,) + total.shape)
-        parts = lax.all_to_all(
-            block, "tm", 0, 0, axis_index_groups=along(stage, count)
-        ).astype(jnp.float32)
-        earlier = (jnp.arange(size, dtype=jnp.int32) < here)[:, None, None]
-        prefix = prefix + jnp.sum(jnp.where(earlier, parts, 0.0), axis=0)
-        total = jnp.sum(parts, axis=0)
-    return prefix
+    x, y, z = place_of(lax.axis_index("tm"))
+    near = jnp.arange(4 * NX, dtype=jnp.int32)
+    far = jnp.arange(NY * NZ // 4, dtype=jnp.int32)
+    member = step_of(near % NX, y // 2 * 2 + near // NX % 2, z // 2 * 2 + near // (2 * NX))
+    target = step_of(x, far % (NY // 2) * 2 + y % 2, far // (NY // 2) * 2 + z % 2)
+    wanted = (member[None, :] <= target[:, None]).astype(jnp.bfloat16)
+    block = jnp.broadcast_to(term.astype(jnp.bfloat16)[None], near.shape + term.shape)
+    block, wanted = lax.optimization_barrier((block, wanted))
+    gathered = lax.all_to_all(
+        block, "tm", 0, 0, axis_index_groups=same(count, lambda x, y, z: (y // 2, z // 2))
+    )
+    sums = lax.dot_general(
+        wanted, gathered, (((1,), (0,)), ((), ())), preferred_element_type=jnp.float32
+    ).astype(jnp.bfloat16)
+    parts = lax.all_to_all(
+        sums, "tm", 0, 0, axis_index_groups=same(count, lambda x, y, z: (x, y % 2, z % 2))
+    )
+    return jnp.sum(parts.astype(jnp.float32), axis=0)
 
 
 def on_device(latents, timesteps, modulation, w_in, w_query, w_key, w_value, w_attn_out, w_final):

time: 75.9 us -> 70.9 us (0.934)
  the two profiles are of different devices: /device:TPU:2 before, /device:TPU:1 now
where the time goes in v2:
time: 70.9 us; the launch traced here: 70 us
  blocking collectives  34.4 us (49%)
  matrix products  15.7 us (22%)
  starting transfers between devices  10.7 us (15%)
  other arithmetic  3.92 us (6%)
  local copies, waits for them, and re-layouts  3.6 us (5%)
  between operations  1.71 us (2%)
    all_to_all x1, blocking collectives, prefix_over_steps(): lax.all_to_all(sums, 'tm', 0, 0, axis_index_groups=same(count, lambda x,...  24 us
    all_to_all x1, blocking collectives, prefix_over_steps(): lax.all_to_all(block, 'tm', 0, 0, axis_index_groups=same(count, lambda x,...  10.4 us
    ppermute x1, starting transfers between devices, on_device(): other_latent = lax.ppermute(own_latent, 'seq', swap)  8.77 us
    dot_general x3, matrix products, project(): jnp.dot(normed, weight, preferred_element_type=jnp.float32)  6.96 us
    sub x1, matrix products, attend_heads(): weights = jnp.exp(scores - row_peak)  3.18 us
    unnamed x12, local copies, waits for them, and re-layouts  2.57 us
    dot_general x1, matrix products, attend_heads(): jnp.einsum('hqk,khd->qhd', weights, values_heads, preferred_element_type=...  2.06 us
    ppermute x1, starting transfers between devices, on_device(): received = lax.ppermute(partial[token_count:], 'seq', swap)  1.93 us
  transfers between devices with their start and end apart: 2, of which 0 were waited for; matrix products, arithmetic and copies ran while one was open for 4% of the time, Pallas kernels for 0%

profile of v2, /device:TPU:1, one launch (start us, length us, event | category | flops | bytes accessed | tf_op | source)
XLA Modules:
  0.0 70.0 jit_solution(8329547698741995824)
XLA Ops:
  0.0 0.0 copy-start
  0.0 0.8 %bitcast_convert_fusion = bf16[64,128]{1,0:T(8,128)(2,1)S(1)} fusion(f32[1,128,64]{1,2,0:T(8,128)} %param.9), kind=kLoop, calls=%fused_computation.80 | loop fusion | flops 8192 | bytes 49152
  0.8 8.8 %collective-permute-start = (bf16[64,128]{1,0:T(8,128)(2,1)S(1)}, bf16[64,128]{1,0:T(8,128)(2,1)S(1)}, u32[]{:S(2)}, u32[]{:S(2)}) collective-permute-start(bf16[64,128]{1,0:T(8,128)(2,1)S(1)} %bitcast_convert_fusion), channel_id=1, source_target_pairs={{0,1},{1,0},{2,3},{3,2},{4,5},{5,4},{6,7},{7,6},{8,9},{9,8},{10,11... | collective-permute-start | bytes 49160 | tf_op jit(solution)/shard_map/ppermute | solution.py:81
  9.6 0.0 copy-done
  9.6 1.2 %fusion.49 = (f32[128]{0:T(128)S(1)}, f32[128,2048]{1,0:T(8,128)S(1)}) fusion(bf16[64,2048]{1,0:T(8,128)(2,1)S(1)} %copy-done, f32[1,128,64]{1,2,0:T(8,128)} %param.9), kind=kOutput, calls=%fused_computation.76 | convolution fusion | flops 33816448 | bytes 1344000 | tf_op jit(solution)/shard_map/dot_general | solution.py:85
  10.8 0.8 %slice_add_fusion = (f32[1,1,2048]{2,0,1:T(1,128)S(1)}, f32[1,1,2048]{2,0,1:T(1,128)S(1)}, f32[1,1,2048]{2,0,1:T(1,128)S(1)}, f32[1,1,2048]{2,0,1:T(1,128)S(1)}, f32[1,1,2048]{2,0,1:T(1,128)S(1)}) fusion(f32[1,5,2048]{2,0,1:T(1,128)} %param.11), kind=kLoop, calls=%fused_computation.40 | loop fusion | flops 4096 | bytes 81920 | tf_op jit(solution)/shard_map/add | solution.py:103
  11.6 0.3 multiply_reduce_fusion.3
  11.8 0.0 collective-permute-done
  11.8 0.4 fusion.50
  12.2 0.0 copy-start.2
  12.3 0.3 multiply_reduce_fusion.2
  12.5 0.5 add_convert_fusion.2
  13.0 1.4 %copy-done.2 = bf16[2048,1024]{1,0:T(8,128)(2,1)S(1)} copy-done((bf16[2048,1024]{1,0:T(8,128)(2,1)S(1)}, bf16[2048,1024]{1,0:T(8,128)(2,1)}, u32[]{:S(2)}) %copy-start.2) | copy-done | bytes 4194328
  14.4 1.3 %convolution_convert_fusion.4 = bf16[256,1024]{1,0:T(8,128)(2,1)S(1)} fusion(bf16[2048,1024]{1,0:T(8,128)(2,1)S(1)} %copy-done.2, bf16[128,2048]{1,0:T(8,128)(2,1)S(1)} %get-tuple-element.17, bf16[128,2048]{1,0:T(8,128)(2,1)S(1)} %get-tuple-element.16), kind=kOutput, calls=%fused_computation.9 | convolution fusion | flops 1076101120 | bytes 5767168 | tf_op jit(solution)/shard_map/dot_general | solution.py:95
  15.7 0.2 copy.21
  15.9 0.0 copy-start.3
  15.9 3.6 %fusion.3 = bf16[32,8,8,128]{3,2,1,0:T(8,128)(2,1)S(1)} fusion(bf16[2048,1024]{1,0:T(8,128)(2,1)} %param.14, bf16[128,2048]{1,0:T(8,128)(2,1)S(1)} %get-tuple-element.17, bf16[128,2048]{1,0:T(8,128)(2,1)S(1)} %get-tuple-element.16), kind=kOutput, calls=%fused_computation.11 | convolution fusion | flops 1076101120 | bytes 5767168 | tf_op jit(solution)/shard_map/dot_general | solution.py:95
  19.5 0.0 copy-done.3
  19.6 2.1 %fusion.2 = bf16[32,8,8,128]{3,2,1,0:T(8,128)(2,1)} fusion(bf16[2048,1024]{1,0:T(8,128)(2,1)S(1)} %copy-done.3, bf16[128,2048]{1,0:T(8,128)(2,1)S(1)} %get-tuple-element.17, bf16[128,2048]{1,0:T(8,128)(2,1)S(1)} %get-tuple-element.16), kind=kOutput, calls=%fused_computation.10 | convolution fusion | flops 1076101120 | bytes 5767168 | tf_op jit(solution)/shard_map/dot_general | solution.py:95
  21.6 3.2 %fusion.51 = (f32[8,256]{1,0:T(8,128)S(1)}, f32[8,256,256]{1,2,0:T(8,128)}) fusion(bf16[32,8,8,128]{3,2,1,0:T(8,128)(2,1)S(1)} %fusion.3, bf16[32,8,8,128]{3,2,1,0:T(8,128)(2,1)} %fusion.2), kind=kOutput, calls=%fused_computation.78 | convolution fusion | flops 135790848 | bytes 3153920 | tf_op jit(solution)/shard_map/sub | solution.py:33
  24.8 0.0 copy-start.4
  24.8 2.1 %convolution_convert_fusion.1 = bf16[8,128,256]{2,1,0:T(8,128)(2,1)S(1)} fusion(bf16[256,8,128]{0,2,1:T(8,128)(2,1)S(1)} %bitcast.72, f32[8,256,256]{1,2,0:T(8,128)} %get-tuple-element.25, f32[8,256]{1,0:T(8,128)S(1)} %get-tuple-element.24), kind=kOutput, calls=%fused_computation.6 | convolution fusion | flops 135528448 | bytes 3153920 | tf_op jit(solution)/shard_map/hqk,khd->qhd/dot_general | solution.py:35
  26.9 0.8 %copy-done.4 = bf16[1024,2048]{1,0:T(8,128)(2,1)S(1)} copy-done((bf16[1024,2048]{1,0:T(8,128)(2,1)S(1)}, bf16[1024,2048]{1,0:T(8,128)(2,1)}, u32[]{:S(2)}) %copy-start.4) | copy-done | bytes 4194328
  27.6 0.0 copy-start.1
  27.6 1.3 %convolution_convert_fusion = bf16[256,2048]{1,0:T(8,128)(2,1)S(1)} fusion(bf16[256,1024]{0,1:T(8,128)(2,1)S(1)} %bitcast.78, bf16[1024,2048]{1,0:T(8,128)(2,1)S(1)} %copy-done.4), kind=kOutput, calls=%fused_computation.1 | convolution fusion | flops 1074266112 | bytes 5767168 | tf_op jit(solution)/shard_map/dot_general | solution.py:98
  29.0 1.9 %collective-permute-start.1 = (bf16[128,2048]{1,0:T(8,128)(2,1)S(1)}, bf16[128,2048]{1,0:T(8,128)(2,1)S(1)}, u32[]{:S(2)}, u32[]{:S(2)}) collective-permute-start(bf16[128,2048]{1,0:T(8,128)(2,1)S(1)} %slice.36), channel_id=1, source_target_pairs={{0,1},{1,0},{2,3},{3,2},{4,5},{5,4},{6,7},{7,6},{8,9},{9,8},{10,11... | collective-permute-start | bytes 1572872 | tf_op jit(solution)/shard_map/ppermute | solution.py:100
  31.0 0.0 copy-done.1
  31.1 0.7 fusion.48
  33.1 0.1 compare_convert_fusion
  33.2 0.0 collective-permute-done.1
  33.2 0.0 copy-start.5
  33.2 0.3 fusion.47
  33.5 0.3 multiply_reduce_fusion.1
  33.8 0.3 copy-done.5
  34.2 0.4 fusion.5
  34.6 10.4 %all_to_all.10 = bf16[16,64,128]{2,1,0:T(8,128)(2,1)S(1)} all-to-all(bf16[16,64,128]{2,1,0:T(8,128)(2,1)S(1)} %broadcast_in_dim.4), channel_id=1, replica_groups={{0,2,4,6,8,10,12,14,64,66,68,70,72,74,76,78},{16,18,20,22,24,26,28,30,8..., dimensions={0} | all-to-all | bytes 524288 | tf_op jit(solution)/shard_map/all_to_all | solution.py:66
  45.0 0.3 convolution_convert_fusion.5
  45.3 0.1 copy.19
  45.3 24.0 %all_to_all.11 = bf16[16,64,128]{2,1,0:T(8,128)(2,1)S(1)} all-to-all(bf16[16,64,128]{2,1,0:T(8,128)(2,1)S(1)} %copy.19), channel_id=1, replica_groups={{0,16,32,48,128,144,160,176,256,272,288,304,384,400,416,432},{2,18,34,5..., dimensions={0} | all-to-all | bytes 524288 | tf_op jit(solution)/shard_map/all_to_all | solution.py:72
  69.3 0.7 convert_reduce_fusion
  (10 shorter events, 0.1 us)
Async XLA Ops:
  0.0 9.6 %copy-start = (bf16[64,2048]{1,0:T(8,128)(2,1)S(1)}, bf16[64,2048]{1,0:T(8,128)(2,1)}, u32[]{:S(2)}) copy-start(bf16[64,2048]{1,0:T(8,128)(2,1)} %param.12) | copy-start | bytes 786436
  0.8 11.0 %collective-permute-start = (bf16[64,128]{1,0:T(8,128)(2,1)S(1)}, bf16[64,128]{1,0:T(8,128)(2,1)S(1)}, u32[]{:S(2)}, u32[]{:S(2)}) collective-permute-start(bf16[64,128]{1,0:T(8,128)(2,1)S(1)} %bitcast_convert_fusion), channel_id=1, source_target_pairs={{0,1},{1,0},{2,3},{3,2},{4,5},{5,4},{6,7},{7,6},{8,9},{9,8},{10,11... | collective-permute-start | bytes 49160 | tf_op jit(solution)/shard_map/ppermute | solution.py:81
  12.2 2.2 %copy-start.2 = (bf16[2048,1024]{1,0:T(8,128)(2,1)S(1)}, bf16[2048,1024]{1,0:T(8,128)(2,1)}, u32[]{:S(2)}) copy-start(bf16[2048,1024]{1,0:T(8,128)(2,1)} %param.15) | copy-start | bytes 12582916
  15.9 3.6 %copy-start.3 = (bf16[2048,1024]{1,0:T(8,128)(2,1)S(1)}, bf16[2048,1024]{1,0:T(8,128)(2,1)}, u32[]{:S(2)}) copy-start(bf16[2048,1024]{1,0:T(8,128)(2,1)} %param.13) | copy-start | bytes 12582916
  24.8 2.8 %copy-start.4 = (bf16[1024,2048]{1,0:T(8,128)(2,1)S(1)}, bf16[1024,2048]{1,0:T(8,128)(2,1)}, u32[]{:S(2)}) copy-start(bf16[1024,2048]{1,0:T(8,128)(2,1)} %param.16) | copy-start | bytes 12582916
  27.6 3.4 %copy-start.1 = (s32[256]{0:T(256)S(1)}, s32[256]{0:T(256)}, u32[]{:S(2)}) copy-start(s32[256]{0:T(256)} %param.10) | copy-start | bytes 3076
  29.0 4.2 %collective-permute-start.1 = (bf16[128,2048]{1,0:T(8,128)(2,1)S(1)}, bf16[128,2048]{1,0:T(8,128)(2,1)S(1)}, u32[]{:S(2)}, u32[]{:S(2)}) collective-permute-start(bf16[128,2048]{1,0:T(8,128)(2,1)S(1)} %slice.36), channel_id=1, source_target_pairs={{0,1},{1,0},{2,3},{3,2},{4,5},{5,4},{6,7},{7,6},{8,9},{9,8},{10,11... | collective-permute-start | bytes 1572872 | tf_op jit(solution)/shard_map/ppermute | solution.py:100
  33.2 1.0 %copy-start.5 = (bf16[2048,64]{0,1:T(8,128)(2,1)S(1)}, bf16[2048,64]{0,1:T(8,128)(2,1)}, u32[]{:S(2)}) copy-start(bf16[2048,64]{0,1:T(8,128)(2,1)} %param.17) | copy-start | bytes 786436

commit v3 on v2

--- a/solution.py
+++ b/solution.py
@@ -1,9 +1,15 @@
 import jax
 import jax.numpy as jnp
 from jax import lax
+from jax.experimental import pallas as pl
+from jax.experimental.pallas import tpu as pltpu
 from jax.sharding import PartitionSpec as P
 
 HEAD_DIM = 128
+PAIR = 2 * HEAD_DIM
+LOG2_E = 1.4426950408889634
+AHEAD = 5
+SKEW = True
 TSCALE = 1024
 NX, NY, NZ = 4, 8, 8
 
@@ -16,26 +22,124 @@
     return center * lax.rsqrt(spread + norm_eps)
 
 
-def modulated(hidden, modulate):
-    return (layer_norm(hidden) * (1.0 + modulate[1]) + modulate[0]).astype(jnp.bfloat16)
-
-
-def attend_heads(queries, keys_all, values_all):
-    token_count = queries.shape[0]
-    local_heads = queries.shape[1] // HEAD_DIM
-    queries = queries.reshape(token_count, local_heads, HEAD_DIM)
-    keys_heads = keys_all.reshape(token_count, local_heads, HEAD_DIM)
-    values_heads = values_all.reshape(token_count, local_heads, HEAD_DIM)
-    scores = jnp.einsum(
-        "qhd,khd->hqk", queries, keys_heads, preferred_element_type=jnp.float32
-    ) * HEAD_DIM ** (-0.5)
-    row_peak = jnp.max(scores, axis=-1, keepdims=True)
-    weights = jnp.exp(scores - row_peak)
-    weights = (weights / jnp.sum(weights, axis=-1, keepdims=True)).astype(jnp.bfloat16)
-    mixed = jnp.einsum(
-        "hqk,khd->qhd", weights, values_heads, preferred_element_type=jnp.float32
-    ).astype(jnp.bfloat16)
-    return mixed.reshape(token_count, local_heads * HEAD_DIM)
+def hidden_of(latent, w_in):
+    return lax.dot_general(
+        latent.astype(jnp.bfloat16), w_in, (((0,), (0,)), ((), ())), preferred_element_type=jnp.float32
+    )
+
+
+def attention_kernel(
+    other_latent, own_latent, modulate, w_in, w_query, w_key, w_value, w_attn_out,
+    keep, send, latent, modulate_held, w_in_held, normed, mixed, w_held, w_out_held, small_sems, sems,
+):
+    half = own_latent.shape[1]
+    small = [
+        pltpu.make_async_copy(own_latent, latent.at[0], small_sems.at[0]),
+        pltpu.make_async_copy(other_latent, latent.at[1], small_sems.at[1]),
+        pltpu.make_async_copy(w_in, w_in_held, small_sems.at[2]),
+        pltpu.make_async_copy(modulate, modulate_held, small_sems.at[3]),
+    ]
+    queue = []
+    for block in range(w_held.shape[0]):
+        for which, weight in enumerate((w_query, w_key, w_value)):
+            queue.append((weight.at[:, pl.ds(block * PAIR, PAIR)], w_held.at[block, which]))
+    for first in range(0, w_attn_out.shape[0], PAIR):
+        rows = pl.ds(first, PAIR)
+        queue.append((w_attn_out.at[rows, :], w_out_held.at[rows, :]))
+    queue = [pltpu.make_async_copy(*ends, sems.at[i]) for i, ends in enumerate(queue)]
+    waited = []
+
+    def arrive():
+        queue[len(waited)].wait()
+        if len(waited) + AHEAD < len(queue):
+            queue[len(waited) + AHEAD].start()
+        waited.append(True)
+
+    for copy in small + queue[:AHEAD]:
+        copy.start()
+    for copy in small:
+        copy.wait()
+
+    for place in range(2):
+        hidden = hidden_of(latent[place], w_in_held[...])
+        shaped = layer_norm(hidden) * (1.0 + modulate_held[1]) + modulate_held[0]
+        normed[place * half : (place + 1) * half, :] = shaped.astype(jnp.bfloat16)
+
+    def project(block, which):
+        return jnp.dot(
+            normed[...], w_held[block, which], preferred_element_type=jnp.float32
+        ).astype(jnp.bfloat16)
+
+    ones = jnp.ones((2 * half, HEAD_DIM), jnp.bfloat16)
+
+    def attend(block, query, key, value):
+        for head in range(PAIR // HEAD_DIM):
+            cols = slice(head * HEAD_DIM, (head + 1) * HEAD_DIM)
+            scores = lax.dot_general(
+                query[:, cols], key[:, cols], (((1,), (1,)), ((), ())), preferred_element_type=jnp.float32
+            )
+            peak = jnp.max(scores, axis=-1, keepdims=True)
+            weights = jnp.exp2((scores - peak) * (HEAD_DIM ** (-0.5) * LOG2_E)).astype(jnp.bfloat16)
+            both = jnp.dot(
+                weights,
+                jnp.concatenate([value[:, cols], ones], axis=1),
+                preferred_element_type=jnp.float32,
+            )
+            first = block * PAIR + head * HEAD_DIM
+            mixed[:, first : first + HEAD_DIM] = (both[:, :HEAD_DIM] / both[:, HEAD_DIM:]).astype(
+                jnp.bfloat16
+            )
+
+    before = None
+    for block in range(w_held.shape[0]):
+        for which in range(3):
+            arrive()
+        projected = [project(block, which) for which in range(3)]
+        if SKEW:
+            if before is not None:
+                attend(block - 1, *before)
+            before = projected
+        else:
+            attend(block, *projected)
+    if SKEW:
+        attend(block, *before)
+    while len(waited) < len(queue):
+        arrive()
+    for first in range(0, keep.shape[1], PAIR):
+        cols = slice(first, first + PAIR)
+        partial = jnp.dot(
+            mixed[...], w_out_held[:, cols], preferred_element_type=jnp.float32
+        ).astype(jnp.bfloat16)
+        keep[:, cols] = partial[:half]
+        send[:, cols] = partial[half:]
+
+
+def attention(other_latent, own_latent, modulate, w_in, w_query, w_key, w_value, w_attn_out):
+    half = own_latent.shape[1]
+    width, cols = w_query.shape
+    blocks = cols // PAIR
+    part = jax.ShapeDtypeStruct((half, width), jnp.bfloat16)
+    return pl.pallas_call(
+        attention_kernel,
+        out_shape=(part, part),
+        in_specs=[pl.BlockSpec(memory_space=pl.ANY)] * 8,
+        out_specs=(pl.BlockSpec(memory_space=pltpu.VMEM),) * 2,
+        scratch_shapes=[
+            pltpu.VMEM((2,) + own_latent.shape, jnp.float32),
+            pltpu.VMEM(modulate.shape, jnp.float32),
+            pltpu.VMEM(w_in.shape, jnp.bfloat16),
+            pltpu.VMEM((2 * half, width), jnp.bfloat16),
+            pltpu.VMEM((2 * half, cols), jnp.bfloat16),
+            pltpu.VMEM((blocks, 3, width, PAIR), jnp.bfloat16),
+            pltpu.VMEM(w_attn_out.shape, jnp.bfloat16),
+            pltpu.SemaphoreType.DMA((4,)),
+            pltpu.SemaphoreType.DMA((4 * blocks,)),
+        ],
+        compiler_params=pltpu.CompilerParams(vmem_limit_bytes=36 * 2**20),
+        cost_estimate=pl.CostEstimate(
+            flops=2 * 2 * half * width * cols * 4, bytes_accessed=2 * width * cols * 4, transcendentals=0
+        ),
+    )(other_latent, own_latent, modulate, w_in, w_query, w_key, w_value, w_attn_out)
 
 
 def same(count, key):
@@ -79,27 +183,17 @@
     swap = [(0, 1), (1, 0)]
     own_latent = latents[0].T
     other_latent = lax.ppermute(own_latent, "seq", swap)
-    modulate = modulation[0]
-
-    def hidden_of(latent):
-        return lax.dot_general(
-            latent.astype(jnp.bfloat16), w_in, (((0,), (0,)), ((), ())), preferred_element_type=jnp.float32
-        )
-
-    own_hidden = hidden_of(own_latent)
-    normed = jnp.concatenate(
-        [modulated(own_hidden, modulate), modulated(hidden_of(other_latent), modulate)]
-    )
-
-    def project(weight):
-        return jnp.dot(normed, weight, preferred_element_type=jnp.float32).astype(jnp.bfloat16)
-
-    head_mixed = attend_heads(project(w_query), project(w_key), project(w_value))
-    partial = jnp.dot(head_mixed, w_attn_out, preferred_element_type=jnp.float32).astype(jnp.bfloat16)
-    token_count = own_hidden.shape[0]
-    received = lax.ppermute(partial[token_count:], "seq", swap)
-    attended = partial[:token_count].astype(jnp.float32) + received.astype(jnp.float32)
-    resid = own_hidden + modulate[2] * attended
+    modulate = jnp.transpose(modulation, (1, 0, 2))
+    there = [
+        pltpu.with_memory_space_constraint(array, pltpu.HBM)
+        for array in (own_latent, modulate, w_in, w_query, w_key, w_value, w_attn_out)
+    ]
+    keep, send = attention(other_latent, *there)
+    received = lax.ppermute(send, "seq", swap)
+    own_latent, keep = lax.optimization_barrier((own_latent, keep))
+    hidden = hidden_of(own_latent, w_in)
+    attended = keep.astype(jnp.float32) + received.astype(jnp.float32)
+    resid = hidden + modulate[2] * attended
     final = (layer_norm(resid) * (1.0 + modulate[4]) + modulate[3]).astype(jnp.bfloat16)
     drift = lax.dot_general(
         w_final, final, (((0,), (1,)), ((), ())), preferred_element_type=jnp.float32

time: 70.9 us -> 62.9 us (0.89)
  matrix products: 15.7 us -> 0.96 us
  Pallas kernels: 0 us -> 10.6 us
  local copies, waits for them, and re-layouts: 3.6 us -> 0.79 us
  other arithmetic: 3.92 us -> 2.1 us
  blocking collectives: 34.4 us -> 35.3 us
    pallas_call x0 -> x1, Pallas kernels: none -> 10.6 us  [attention(): pl.pallas_call(attention_kernel, out_shape=(part, part), in_specs=[pl.Blo...]
    dot_general x5 -> x0, matrix products: 10.3 us -> none  [the longest x3 6.96 us: project(): jnp.dot(normed, weight, preferred_element_type=jnp.float32)]
    sub x1 -> x0, matrix products: 3.18 us -> none  [attend_heads(): weights = jnp.exp(scores - row_peak)]
    unnamed x12 -> x8, local copies, waits for them, and re-layouts: 2.57 us -> 0.02 us
    dot_general x2 -> x1, matrix products: 1.55 us -> 0.32 us  [hidden_of(): lax.dot_general(latent.astype(jnp.bfloat16), w_in, (((0,), (0,)), ((), ()...]
    unnamed x1 -> x0, other arithmetic: 0.8 us -> none
  transfers between devices with their start and end apart: 2 -> 2, of which waited for: 0 -> 1; matrix products, arithmetic and copies ran while one was open for 4% -> 3% of each run, Pallas kernels for 0% -> 0%
where the time goes in v3:
time: 62.9 us; the launch traced here: 62.6 us
  blocking collectives  35.3 us (56%)
  starting transfers between devices  11.2 us (18%)
  Pallas kernels  10.6 us (17%)
  other arithmetic  2.1 us (3%)
  between operations  1.51 us (2%)
  matrix products  0.96 us (2%)
  local copies, waits for them, and re-layouts  0.79 us (1%)
    all_to_all x1, blocking collectives, prefix_over_steps(): lax.all_to_all(sums, 'tm', 0, 0, axis_index_groups=same(count, lambda x,...  24.6 us
    all_to_all x1, blocking collectives, prefix_over_steps(): lax.all_to_all(block, 'tm', 0, 0, axis_index_groups=same(count, lambda x,...  10.7 us
    pallas_call x1, Pallas kernels, attention(): pl.pallas_call(attention_kernel, out_shape=(part, part), in_specs=[pl.Blo...  10.6 us
    ppermute x1, starting transfers between devices, on_device(): other_latent = lax.ppermute(own_latent, 'seq', swap)  8.91 us
    ppermute x1, starting transfers between devices, on_device(): received = lax.ppermute(send, 'seq', swap)  2.26 us
  transfers between devices with their start and end apart: 2, of which 1 were waited for; matrix products, arithmetic and copies ran while one was open for 3% of the time, Pallas kernels for 0%

profile of v3, /device:TPU:1, one launch (start us, length us, event | category | flops | bytes accessed | tf_op | source)
XLA Modules:
  0.0 62.6 jit_solution(2152897033892170609)
XLA Ops:
  0.0 0.0 copy-start
  0.0 8.9 %collective-permute-start = (f32[64,128]{1,0:T(8,128)}, f32[64,128]{1,0:T(8,128)S(1)}, u32[]{:S(2)}, u32[]{:S(2)}) collective-permute-start(f32[64,128]{1,0:T(8,128)} %bitcast.19), channel_id=1, source_target_pairs={{0,1},{1,0},{2,3},{3,2},{4,5},{5,4},{6,7},{7,6},{8,9},{9,8},{10,11... | collective-permute-start | bytes 98312 | tf_op jit(solution)/shard_map/ppermute | solution.py:185
  8.9 0.7 %slice_add_fusion = (f32[1,1,2048]{2,0,1:T(1,128)S(1)}, f32[1,1,2048]{2,0,1:T(1,128)S(1)}, f32[1,1,2048]{2,0,1:T(1,128)S(1)}) fusion(f32[1,5,2048]{2,0,1:T(1,128)} %param.11), kind=kLoop, calls=%fused_computation.15 | loop fusion | flops 2048 | bytes 49152 | tf_op jit(solution)/shard_map/add | solution.py:197
  9.8 0.2 collective-permute-done.other_latent
  10.0 0.0 copy-start.3
  10.0 0.0 copy-start.1
  10.0 0.0 copy-start.2
  10.0 10.6 %shard_map.91 = (bf16[128,2048]{1,0:T(8,128)(2,1)S(1)}, bf16[128,2048]{1,0:T(8,128)(2,1)S(1)}) custom-call(f32[64,128]{1,0:T(8,128)S(1)} %collective-permute-done.other_latent, f32[64,128]{1,0:T(8,128)} %bitcast.20, f32[5,1,2048]{2,1,0:T(1,128)} %bitcast.22, bf16[64,2048]{1,0:T(8,128)(2,1)} %w_in.1, bf16[2048,1024]{1,0:T(8,128)(2,1)} %w_query.1, ...), custom_call_target="tpu_custom_call" | custom-call | flops 4294967296 | bytes 16777216 | tf_op jit(solution)/shard_map/pallas_call | solution.py:122
  20.6 2.3 %collective-permute-start.1 = (bf16[128,2048]{1,0:T(8,128)(2,1)S(1)}, bf16[128,2048]{1,0:T(8,128)(2,1)S(1)}, u32[]{:S(2)}, u32[]{:S(2)}) collective-permute-start(bf16[128,2048]{1,0:T(8,128)(2,1)S(1)} %get-tuple-element.14), channel_id=1, source_target_pairs={{0,1},{1,0},{2,3},{3,2},{4,5},{5,4},{6,7},{7,6},{8,9},{9,8},{10,11... | collective-permute-start | bytes 1572872 | tf_op jit(solution)/shard_map/ppermute | solution.py:192
  22.9 0.0 copy-done.3
  22.9 0.7 %fusion.18 = (f32[1]{0:T(128)}, f32[1]{0:T(128)}) fusion(f32[256]{0:T(256)S(1)} %convert_element_type.30, s32[]{:T(128)S(6)} %select_n.93, s32[]{:T(128)S(6)} %select_n.91), kind=kLoop, calls=%fused_computation.40 | loop fusion | bytes 24 | tf_op jit(solution)/shard_map/dynamic_slice | solution.py:204
  24.9 0.1 compare_convert_fusion
  24.9 0.0 copy-done.1
  24.9 0.0 copy-done.2
  24.9 0.3 fusion.7
  25.3 0.0 collective-permute-done.1
  25.3 0.3 fusion.17
  25.6 0.3 multiply_reduce_fusion
  25.9 0.0 copy-done
  25.9 0.4 fusion.1
  26.4 10.7 %all_to_all.10 = bf16[16,64,128]{2,1,0:T(8,128)(2,1)S(1)} all-to-all(bf16[16,64,128]{2,1,0:T(8,128)(2,1)S(1)} %broadcast_in_dim.4), channel_id=1, replica_groups={{0,2,4,6,8,10,12,14,64,66,68,70,72,74,76,78},{16,18,20,22,24,26,28,30,8..., dimensions={0} | all-to-all | bytes 524288 | tf_op jit(solution)/shard_map/all_to_all | solution.py:170
  37.0 0.3 convolution_convert_fusion
  37.3 0.1 copy.11
  37.4 24.6 %all_to_all.11 = bf16[16,64,128]{2,1,0:T(8,128)(2,1)S(1)} all-to-all(bf16[16,64,128]{2,1,0:T(8,128)(2,1)S(1)} %copy.11), channel_id=1, replica_groups={{0,16,32,48,128,144,160,176,256,272,288,304,384,400,416,432},{2,18,34,5..., dimensions={0} | all-to-all | bytes 524288 | tf_op jit(solution)/shard_map/all_to_all | solution.py:176
  62.0 0.7 %convert_reduce_fusion = f32[64,128]{1,0:T(8,128)} fusion(bf16[16,64,128]{2,1,0:T(8,128)(2,1)S(1)} %all_to_all.11), kind=kLoop, calls=%fused_computation.7 | loop fusion | flops 253952 | bytes 294912 | tf_op jit(solution)/shard_map/reduce_sum | solution.py:179
  (5 shorter events, 0.1 us)
Async XLA Ops:
  0.0 25.9 %copy-start = (bf16[2048,64]{0,1:T(8,128)(2,1)S(1)}, bf16[2048,64]{0,1:T(8,128)(2,1)}, u32[]{:S(2)}) copy-start(bf16[2048,64]{0,1:T(8,128)(2,1)} %param.17) | copy-start | bytes 786436
  0.0 10.0 %collective-permute-start = (f32[64,128]{1,0:T(8,128)}, f32[64,128]{1,0:T(8,128)S(1)}, u32[]{:S(2)}, u32[]{:S(2)}) collective-permute-start(f32[64,128]{1,0:T(8,128)} %bitcast.19), channel_id=1, source_target_pairs={{0,1},{1,0},{2,3},{3,2},{4,5},{5,4},{6,7},{7,6},{8,9},{9,8},{10,11... | collective-permute-start | bytes 98312 | tf_op jit(solution)/shard_map/ppermute | solution.py:185
  10.0 12.9 %copy-start.3 = (s32[256]{0:T(256)S(1)}, s32[256]{0:T(256)}, u32[]{:S(2)}) copy-start(s32[256]{0:T(256)} %param.10) | copy-start | bytes 3076
  10.0 15.0 %copy-start.1 = (bf16[64,2048]{1,0:T(8,128)(2,1)S(1)}, bf16[64,2048]{1,0:T(8,128)(2,1)}, u32[]{:S(2)}) copy-start(bf16[64,2048]{1,0:T(8,128)(2,1)} %w_in.1) | copy-start | bytes 786436
  10.0 15.0 %copy-start.2 = (f32[1,128,64]{1,2,0:T(8,128)S(1)}, f32[1,128,64]{1,2,0:T(8,128)}, u32[]{:S(2)}) copy-start(f32[1,128,64]{1,2,0:T(8,128)} %param.9) | copy-start | bytes 98308
  20.6 4.7 %collective-permute-start.1 = (bf16[128,2048]{1,0:T(8,128)(2,1)S(1)}, bf16[128,2048]{1,0:T(8,128)(2,1)S(1)}, u32[]{:S(2)}, u32[]{:S(2)}) collective-permute-start(bf16[128,2048]{1,0:T(8,128)(2,1)S(1)} %get-tuple-element.14), channel_id=1, source_target_pairs={{0,1},{1,0},{2,3},{3,2},{4,5},{5,4},{6,7},{7,6},{8,9},{9,8},{10,11... | collective-permute-start | bytes 1572872 | tf_op jit(solution)/shard_map/ppermute | solution.py:192

commit v4 on v3

v4 whole, which is shorter than its diff:
```python
import jax
import jax.numpy as jnp
from jax import lax
from jax.experimental import pallas as pl
from jax.experimental.pallas import tpu as pltpu
from jax.sharding import PartitionSpec as P

HEAD_DIM = 128
PAIR = 2 * HEAD_DIM
LOG2_E = 1.4426950408889634
AHEAD = 5
TSCALE = 1024
NX, NY, NZ = 4, 8, 8

norm_eps = 1e-06


def layer_norm(values):
    center = values - jnp.mean(values, axis=-1, keepdims=True)
    spread = jnp.mean(center * center, axis=-1, keepdims=True)
    return center * lax.rsqrt(spread + norm_eps)


def hidden_of(latent, w_in):
    return lax.dot_general(
        latent.astype(jnp.bfloat16), w_in, (((0,), (0,)), ((), ())), preferred_element_type=jnp.float32
    )


def shaped(hidden, gain, shift):
    return (layer_norm(hidden) * gain + shift).astype(jnp.bfloat16)


def front_kernel(
    own_latent, modulate, w_in, timesteps, w_query, w_key, w_value,
    normed, first, w_in_held, modulate_held, latent, timesteps_held, small_sems, sems,
):
    small = [
        pltpu.make_async_copy(own_latent, latent, small_sems.at[0]),
        pltpu.make_async_copy(w_in, w_in_held, small_sems.at[1]),
        pltpu.make_async_copy(modulate, modulate_held, small_sems.at[2]),
        pltpu.make_async_copy(timesteps, timesteps_held, small_sems.at[3]),
    ]
    weights = [
        pltpu.make_async_copy(
            weight.at[:, pl.ds(0, PAIR)], first.at[which], sems.at[which]
        )
        for which, weight in enumerate((w_query, w_key, w_value))
    ]
    for copy in small + weights:
        copy.start()
    for copy in small:
        copy.wait()
    normed[...] = shaped(hidden_of(latent[...], w_in_held[...]), 1.0 + modulate_held[1], modulate_held[0])
    for copy in weights:
        copy.wait()


def front(own_latent, modulate, w_in, timesteps, w_query, w_key, w_value):
    half = own_latent.shape[1]
    width = w_in.shape[1]
    return pl.pallas_call(
        front_kernel,
        out_shape=(
            jax.ShapeDtypeStruct((half, width), jnp.bfloat16),
            jax.ShapeDtypeStruct((3, width, PAIR), jnp.bfloat16),
            jax.ShapeDtypeStruct(w_in.shape, jnp.bfloat16),
            jax.ShapeDtypeStruct(modulate.shape, jnp.float32),
            jax.ShapeDtypeStruct(own_latent.shape, jnp.float32),
            jax.ShapeDtypeStruct(timesteps.shape, jnp.int32),
        ),
        in_specs=[pl.BlockSpec(memory_space=pl.ANY)] * 7,
        out_specs=(pl.BlockSpec(memory_space=pltpu.VMEM),) * 6,
        scratch_shapes=[
            pltpu.SemaphoreType.DMA((4,)),
            pltpu.SemaphoreType.DMA((3,)),
        ],
        compiler_params=pltpu.CompilerParams(vmem_limit_bytes=24 * 2**20),
        cost_estimate=pl.CostEstimate(
            flops=2 * half * width * w_in.shape[0], bytes_accessed=6 * width * PAIR, transcendentals=0
        ),
    )(own_latent, modulate, w_in, timesteps, w_query, w_key, w_value)


def attention_kernel(
    other_latent, own_normed, first, w_in, modulate, w_query, w_key, w_value, w_attn_out,
    send, own_mixed, w_out_held, normed, mixed, w_held, sems,
):
    half = other_latent.shape[1]
    blocks = 1 + w_held.shape[0]
    queue = []
    for block in range(1, blocks):
        for which, weight in enumerate((w_query, w_key, w_value)):
            queue.append((weight.at[:, pl.ds(block * PAIR, PAIR)], w_held.at[block - 1, which]))
    for row in range(0, w_attn_out.shape[0], PAIR):
        rows = pl.ds(row, PAIR)
        queue.append((w_attn_out.at[rows, :], w_out_held.at[rows, :]))
    queue = [pltpu.make_async_copy(*ends, sems.at[i]) for i, ends in enumerate(queue)]
    waited = []

    def arrive():
        queue[len(waited)].wait()
        if len(waited) + AHEAD < len(queue):
            queue[len(waited) + AHEAD].start()
        waited.append(True)

    for copy in queue[:AHEAD]:
        copy.start()

    normed[:half, :] = own_normed[...]
    normed[half:, :] = shaped(hidden_of(other_latent[...], w_in[...]), 1.0 + modulate[1], modulate[0])

    def project(block, which):
        weight = first[which] if block == 0 else w_held[block - 1, which]
        return jnp.dot(normed[...], weight, preferred_element_type=jnp.float32).astype(jnp.bfloat16)

    ones = jnp.ones((2 * half, HEAD_DIM), jnp.bfloat16)

    def attend(block, query, key, value):
        for head in range(PAIR // HEAD_DIM):
            cols = slice(head * HEAD_DIM, (head + 1) * HEAD_DIM)
            scores = lax.dot_general(
                query[:, cols], key[:, cols], (((1,), (1,)), ((), ())), preferred_element_type=jnp.float32
            )
            peak = jnp.max(scores, axis=-1, keepdims=True)
            weights = jnp.exp2((scores - peak) * (HEAD_DIM ** (-0.5) * LOG2_E)).astype(jnp.bfloat16)
            both = jnp.dot(
                weights,
                jnp.concatenate([value[:, cols], ones], axis=1),
                preferred_element_type=jnp.float32,
            )
            result = (both[:, :HEAD_DIM] / both[:, HEAD_DIM:]).astype(jnp.bfloat16)
            col = block * PAIR + head * HEAD_DIM
            own_mixed[:, col : col + HEAD_DIM] = result[:half]
            mixed[:, col : col + HEAD_DIM] = result[half:]

    before = [project(0, which) for which in range(3)]
    for block in range(1, blocks):
        for which in range(3):
            arrive()
        projected = [project(block, which) for which in range(3)]
        attend(block - 1, *before)
        before = projected
    attend(blocks - 1, *before)
    while len(waited) < len(queue):
        arrive()
    for col in range(0, send.shape[1], PAIR):
        cols = slice(col, col + PAIR)
        send[:, cols] = jnp.dot(
            mixed[...], w_out_held[:, cols], preferred_element_type=jnp.float32
        ).astype(jnp.bfloat16)


def attention(other_latent, own_normed, first, w_in, modulate, w_query, w_key, w_value, w_attn_out):
    half = other_latent.shape[1]
    width, cols = w_query.shape
    blocks = cols // PAIR
    return pl.pallas_call(
        attention_kernel,
        out_shape=(
            jax.ShapeDtypeStruct((half, width), jnp.bfloat16),
            jax.ShapeDtypeStruct((half, cols), jnp.bfloat16),
            jax.ShapeDtypeStruct(w_attn_out.shape, jnp.bfloat16),
        ),
        in_specs=[pl.BlockSpec(memory_space=pltpu.VMEM)] * 5 + [pl.BlockSpec(memory_space=pl.ANY)] * 4,
        out_specs=(pl.BlockSpec(memory_space=pltpu.VMEM),) * 3,
        scratch_shapes=[
            pltpu.VMEM((2 * half, width), jnp.bfloat16),
            pltpu.VMEM((half, cols), jnp.bfloat16),
            pltpu.VMEM((blocks - 1, 3, width, PAIR), jnp.bfloat16),
            pltpu.SemaphoreType.DMA((4 * blocks - 3,)),
        ],
        compiler_params=pltpu.CompilerParams(vmem_limit_bytes=32 * 2**20),
        cost_estimate=pl.CostEstimate(
            flops=2 * 2 * half * width * cols * 4, bytes_accessed=2 * width * cols * 4, transcendentals=0
        ),
    )(other_latent, own_normed, first, w_in, modulate, w_query, w_key, w_value, w_attn_out)


def own_rows_kernel(own_latent, w_in, modulate, timesteps, chosen, own_mixed, w_attn_out, out, step_size):
    times = jnp.sum(timesteps[...].astype(jnp.float32) * chosen[...], axis=1, keepdims=True)
    step_size[...] = jnp.broadcast_to((times[1:] - times[:1]) / TSCALE, step_size.shape)
    for col in range(0, out.shape[1], PAIR):
        cols = slice(col, col + PAIR)
        partial = jnp.dot(
            own_mixed[...], w_attn_out[:, cols], preferred_element_type=jnp.float32
        ).astype(jnp.bfloat16)
        out[:, cols] = hidden_of(own_latent[...], w_in[:, cols]) + modulate[2, :, cols] * partial.astype(
            jnp.float32
        )


def own_rows(own_latent, w_in, modulate, timesteps, chosen, own_mixed, w_attn_out):
    half, cols = own_mixed.shape
    width = w_attn_out.shape[1]
    return pl.pallas_call(
        own_rows_kernel,
        out_shape=(
            jax.ShapeDtypeStruct((half, width), jnp.float32),
            jax.ShapeDtypeStruct((1, half), jnp.float32),
        ),
        in_specs=[pl.BlockSpec(memory_space=pltpu.VMEM)] * 7,
        out_specs=(pl.BlockSpec(memory_space=pltpu.VMEM),) * 2,
        compiler_params=pltpu.CompilerParams(vmem_limit_bytes=24 * 2**20),
        cost_estimate=pl.CostEstimate(
            flops=2 * half * width * cols, bytes_accessed=4 * half * width, transcendentals=0
        ),
    )(own_latent, w_in, modulate, timesteps, chosen, own_mixed, w_attn_out)


def same(count, key):
    groups = {}
    for step in range(count):
        groups.setdefault(key(*place_of(step)), []).append(step)
    return list(groups.values())


def place_of(step):
    return step % NX, step // NX % NY, step // (NX * NY)


def step_of(x, y, z):
    return (z * NY + y) * NX + x


def prefix_over_steps(term):
    count = lax.axis_size("tm")
    x, y, z = place_of(lax.axis_index("tm"))
    near = jnp.arange(4 * NX, dtype=jnp.int32)
    far = jnp.arange(NY * NZ // 4, dtype=jnp.int32)
    member = step_of(near % NX, y // 2 * 2 + near // NX % 2, z // 2 * 2 + near // (2 * NX))
    target = step_of(x, far % (NY // 2) * 2 + y % 2, far // (NY // 2) * 2 + z % 2)
    wanted = (member[None, :] <= target[:, None]).astype(jnp.bfloat16)
    block = jnp.broadcast_to(term.astype(jnp.bfloat16)[None], near.shape + term.shape)
    block, wanted = lax.optimization_barrier((block, wanted))
    gathered = lax.all_to_all(
        block, "tm", 0, 0, axis_index_groups=same(count, lambda x, y, z: (y // 2, z // 2))
    )
    sums = lax.dot_general(
        wanted, gathered, (((1,), (0,)), ((), ())), preferred_element_type=jnp.float32
    ).astype(jnp.bfloat16)
    parts = lax.all_to_all(
        sums, "tm", 0, 0, axis_index_groups=same(count, lambda x, y, z: (x, y % 2, z % 2))
    )
    return jnp.sum(parts.astype(jnp.float32), axis=0)


def on_device(latents, timesteps, modulation, w_in, w_query, w_key, w_value, w_attn_out, w_final):
    swap = [(0, 1), (1, 0)]
    own_latent = latents[0].T
    other_latent = lax.ppermute(own_latent, "seq", swap)
    modulate = jnp.transpose(modulation, (1, 0, 2))
    there = [
        pltpu.with_memory_space_constraint(array, pltpu.HBM)
        for array in (own_latent, modulate, w_in, timesteps[None], w_query, w_key, w_value, w_attn_out)
    ]
    own_normed, first, w_in_held, modulate, own_latent, times = front(*there[:7])
    send, own_mixed, w_out_held = attention(
        other_latent, own_normed, first, w_in_held, modulate, *there[4:]
    )
    received = lax.ppermute(send, "seq", swap)
    ahead = jnp.arange(timesteps.shape[0], dtype=jnp.int32)[None] - lax.axis_index("tm")
    chosen = (ahead == jnp.arange(2, dtype=jnp.int32)[:, None]).astype(jnp.float32)
    own_part, step_size = own_rows(
        own_latent, w_in_held, modulate, times, chosen, own_mixed, w_out_held
    )
    resid = own_part + modulate[2] * received.astype(jnp.float32)
    final = (layer_norm(resid) * (1.0 + modulate[4]) + modulate[3]).astype(jnp.bfloat16)
    drift = lax.dot_general(
        w_final, final, (((0,), (1,)), ((), ())), preferred_element_type=jnp.float32
    )
    return prefix_over_steps(step_size * drift).T[None]


def solution(mesh):
    placed = (
        P("tm", "seq", None),
        P(),
        P("tm", None, None),
        P(),
        P(None, "seq"),
        P(None, "seq"),
        P(None, "seq"),
        P("seq", None),
        P(),
    )
    return jax.shard_map(
        on_device, mesh=mesh, in_specs=placed, out_specs=P("tm", "seq", None), check_vma=False
    )
```

time: 62.9 us -> 60.7 us (0.965)
  between operations: 1.51 us -> 0.21 us
  other arithmetic: 2.1 us -> 1.35 us
  waiting for transfers between devices: 0.21 us -> 0.9 us
  local copies, waits for them, and re-layouts: 0.79 us -> 0.12 us
    ppermute x1, waiting for transfers between devices: 0.01 us -> 0.9 us  [on_device(): received = lax.ppermute(send, 'seq', swap)]
    add x1 -> x0, other arithmetic: 0.74 us -> none  [on_device(): 1.0 + modulate[4]]
    dynamic_slice x1 -> x0, local copies, waits for them, and re-layouts: 0.66 us -> none  [on_device(): current = time_values[step_index]]
    pallas_call x1 -> x3, Pallas kernels: 10.6 us -> 11 us  [the longest x1 7.89 us: attention(): pl.pallas_call(attention_kernel, out_shape=(jax.ShapeDtypeStruct((half, w...]
  transfers between devices with their start and end apart: 2 -> 2, of which waited for: 1 -> 1; matrix products, arithmetic and copies ran while one was open for 3% -> 0% of each run, Pallas kernels for 0% -> 5%
where the time goes in v4:
time: 60.7 us; the launch traced here: 60.4 us
  blocking collectives  35.3 us (58%)
  Pallas kernels  11 us (18%)
  starting transfers between devices  10.8 us (18%)
  other arithmetic  1.35 us (2%)
  waiting for transfers between devices  0.9 us (1%)
  matrix products  0.72 us (1%)
    all_to_all x1, blocking collectives, prefix_over_steps(): lax.all_to_all(sums, 'tm', 0, 0, axis_index_groups=same(count, lambda x,...  24.6 us
    all_to_all x1, blocking collectives, prefix_over_steps(): lax.all_to_all(block, 'tm', 0, 0, axis_index_groups=same(count, lambda x,...  10.7 us
    ppermute x1, starting transfers between devices, on_device(): other_latent = lax.ppermute(own_latent, 'seq', swap)  8.91 us
    pallas_call x1, Pallas kernels, attention(): pl.pallas_call(attention_kernel, out_shape=(jax.ShapeDtypeStruct((half, w...  7.89 us
    pallas_call x1, Pallas kernels, front(): pl.pallas_call(front_kernel, out_shape=(jax.ShapeDtypeStruct((half, width...  2.17 us
    ppermute x1, starting transfers between devices, on_device(): received = lax.ppermute(send, 'seq', swap)  1.93 us
  transfers between devices with their start and end apart: 2, of which 1 were waited for; matrix products, arithmetic and copies ran while one was open for 0% of the time, Pallas kernels for 5%

profile of v4, /device:TPU:1, one launch (start us, length us, event | category | flops | bytes accessed | tf_op | source)
XLA Modules:
  0.0 60.4 jit_solution(2006648148568672541)
XLA Ops:
  0.0 0.0 copy-start
  0.0 8.9 %collective-permute-start = (f32[64,128]{1,0:T(8,128)}, f32[64,128]{1,0:T(8,128)S(1)}, u32[]{:S(2)}, u32[]{:S(2)}) collective-permute-start(f32[64,128]{1,0:T(8,128)} %bitcast.23), channel_id=1, source_target_pairs={{0,1},{1,0},{2,3},{3,2},{4,5},{5,4},{6,7},{7,6},{8,9},{9,8},{10,11... | collective-permute-start | bytes 98312 | tf_op jit(solution)/shard_map/ppermute | solution.py:251
  9.0 0.1 compare_convert_fusion
  9.1 2.2 %shard_map.91 = (bf16[128,2048]{1,0:T(8,128)(2,1)S(1)}, bf16[3,2048,256]{2,1,0:T(8,128)(2,1)S(1)}, bf16[64,2048]{1,0:T(8,128)(2,1)S(1)}, f32[5,1,2048]{2,1,0:T(1...) custom-call(f32[64,128]{1,0:T(8,128)} %bitcast.24, f32[5,1,2048]{2,1,0:T(1,128)} %bitcast.22, ...), custom_call_target="tpu_custom_call" | custom-call | flops 33554432 | bytes 3145728 | tf_op jit(solution)/shard_map/pallas_call | solution.py:62
  11.3 0.0 collective-permute-done.other_latent
  11.3 7.9 %shard_map.92 = (bf16[128,2048]{1,0:T(8,128)(2,1)S(1)}, bf16[128,1024]{1,0:T(8,128)(2,1)S(1)}, bf16[1024,2048]{1,0:T(8,128)(2,1)S(1)}) custom-call(f32[64,128]{1,0:T(8,128)S(1)} %collective-permute-done.other_latent, bf16[128,2048]{1,0:T(8,128)(2,1)S(1)} %get-tuple-element.22.own_normed, bf16[3,2048,256]{2,1,0:T(8,128)(2,1)S(1)} %get-tuple-element.23.first, ...), custom_call_target="tpu_custom_call" | custom-call | flops 4294967296 | bytes 16777216 | tf_op jit(solution)/shard_map/pallas_call | solution.py:158
  19.2 1.9 %collective-permute-start.1 = (bf16[128,2048]{1,0:T(8,128)(2,1)S(1)}, bf16[128,2048]{1,0:T(8,128)(2,1)S(1)}, u32[]{:S(2)}, u32[]{:S(2)}) collective-permute-start(bf16[128,2048]{1,0:T(8,128)(2,1)S(1)} %get-tuple-element.28), channel_id=1, source_target_pairs={{0,1},{1,0},{2,3},{3,2},{4,5},{5,4},{6,7},{7,6},{8,9},{9,8},{10,11... | collective-permute-start | bytes 1572872 | tf_op jit(solution)/shard_map/ppermute | solution.py:261
  21.2 0.9 %shard_map.93 = (f32[128,2048]{1,0:T(8,128)S(1)}, f32[1,128]{1,0:T(1,128)S(1)}) custom-call(f32[64,128]{1,0:T(8,128)S(1)} %get-tuple-element.18.own_latent, bf16[64,2048]{1,0:T(8,128)(2,1)S(1)} %get-tuple-element.19.w_in, f32[5,1,2048]{2,1,0:T(1,128)S(1)} %get-tuple-element.20.modulate, s32[1,256]{1,0:T(1,128)S(1)} %get-tuple-element.21.timesteps, ...), custom_call_target="tpu_custom_call" | custom-call | flops 536870912 | bytes 1048576 | tf_op jit(solution)/shard_map/pallas_call | solution.py:196
  22.1 0.9 %collective-permute-done.1 = bf16[128,2048]{1,0:T(8,128)(2,1)S(1)} collective-permute-done((bf16[128,2048]{1,0:T(8,128)(2,1)S(1)}, bf16[128,2048]{1,0:T(8,128)(2,1)S(1)}, u32[]{:S(2)}, u32[]{:S(2)}) %collective-permute-start.1) | collective-permute-done | bytes 524320 | tf_op jit(solution)/shard_map/ppermute | solution.py:261
  23.0 0.2 fusion.6
  23.3 0.3 multiply_reduce_fusion
  23.6 0.0 copy-done
  23.6 0.5 fusion.1
  24.1 10.7 %all_to_all.10 = bf16[16,64,128]{2,1,0:T(8,128)(2,1)S(1)} all-to-all(bf16[16,64,128]{2,1,0:T(8,128)(2,1)S(1)} %broadcast_in_dim.7), channel_id=1, replica_groups={{0,2,4,6,8,10,12,14,64,66,68,70,72,74,76,78},{16,18,20,22,24,26,28,30,8..., dimensions={0} | all-to-all | bytes 524288 | tf_op jit(solution)/shard_map/all_to_all | solution.py:236
  34.8 0.3 convolution_convert_fusion
  35.1 0.1 copy.11
  35.1 24.6 %all_to_all.11 = bf16[16,64,128]{2,1,0:T(8,128)(2,1)S(1)} all-to-all(bf16[16,64,128]{2,1,0:T(8,128)(2,1)S(1)} %copy.11), channel_id=1, replica_groups={{0,16,32,48,128,144,160,176,256,272,288,304,384,400,416,432},{2,18,34,5..., dimensions={0} | all-to-all | bytes 524288 | tf_op jit(solution)/shard_map/all_to_all | solution.py:242
  59.8 0.7 %convert_reduce_fusion = f32[64,128]{1,0:T(8,128)} fusion(bf16[16,64,128]{2,1,0:T(8,128)(2,1)S(1)} %all_to_all.11), kind=kLoop, calls=%fused_computation.7 | loop fusion | flops 253952 | bytes 294912 | tf_op jit(solution)/shard_map/reduce_sum | solution.py:245
  (7 shorter events, 0.1 us)
Async XLA Ops:
  0.0 23.6 %copy-start = (bf16[2048,64]{0,1:T(8,128)(2,1)S(1)}, bf16[2048,64]{0,1:T(8,128)(2,1)}, u32[]{:S(2)}) copy-start(bf16[2048,64]{0,1:T(8,128)(2,1)} %param.17) | copy-start | bytes 786436
  0.0 11.3 %collective-permute-start = (f32[64,128]{1,0:T(8,128)}, f32[64,128]{1,0:T(8,128)S(1)}, u32[]{:S(2)}, u32[]{:S(2)}) collective-permute-start(f32[64,128]{1,0:T(8,128)} %bitcast.23), channel_id=1, source_target_pairs={{0,1},{1,0},{2,3},{3,2},{4,5},{5,4},{6,7},{7,6},{8,9},{9,8},{10,11... | collective-permute-start | bytes 98312 | tf_op jit(solution)/shard_map/ppermute | solution.py:251
  19.2 3.8 %collective-permute-start.1 = (bf16[128,2048]{1,0:T(8,128)(2,1)S(1)}, bf16[128,2048]{1,0:T(8,128)(2,1)S(1)}, u32[]{:S(2)}, u32[]{:S(2)}) collective-permute-start(bf16[128,2048]{1,0:T(8,128)(2,1)S(1)} %get-tuple-element.28), channel_id=1, source_target_pairs={{0,1},{1,0},{2,3},{3,2},{4,5},{5,4},{6,7},{7,6},{8,9},{9,8},{10,11... | collective-permute-start | bytes 1572872 | tf_op jit(solution)/shard_map/ppermute | solution.py:261

commit v5 on v4

--- a/solution.py
+++ b/solution.py
@@ -8,7 +8,6 @@
 HEAD_DIM = 128
 PAIR = 2 * HEAD_DIM
 LOG2_E = 1.4426950408889634
-AHEAD = 5
 TSCALE = 1024
 NX, NY, NZ = 4, 8, 8
 
@@ -32,7 +31,7 @@
 
 
 def front_kernel(
-    own_latent, modulate, w_in, timesteps, w_query, w_key, w_value,
+    own_latent, modulate, w_in, timesteps, w_query, w_key,
     normed, first, w_in_held, modulate_held, latent, timesteps_held, small_sems, sems,
 ):
     small = [
@@ -45,10 +44,12 @@
         pltpu.make_async_copy(
             weight.at[:, pl.ds(0, PAIR)], first.at[which], sems.at[which]
         )
-        for which, weight in enumerate((w_query, w_key, w_value))
+        for which, weight in enumerate((w_query, w_key))
     ]
-    for copy in small + weights:
+    for copy in small:
         copy.start()
+    for copy in weights:
+        copy.start(priority=1)
     for copy in small:
         copy.wait()
     normed[...] = shaped(hidden_of(latent[...], w_in_held[...]), 1.0 + modulate_held[1], modulate_held[0])
@@ -56,94 +57,122 @@
         copy.wait()
 
 
-def front(own_latent, modulate, w_in, timesteps, w_query, w_key, w_value):
+def front(own_latent, modulate, w_in, timesteps, w_query, w_key):
     half = own_latent.shape[1]
     width = w_in.shape[1]
     return pl.pallas_call(
         front_kernel,
         out_shape=(
             jax.ShapeDtypeStruct((half, width), jnp.bfloat16),
-            jax.ShapeDtypeStruct((3, width, PAIR), jnp.bfloat16),
+            jax.ShapeDtypeStruct((2, width, PAIR), jnp.bfloat16),
             jax.ShapeDtypeStruct(w_in.shape, jnp.bfloat16),
             jax.ShapeDtypeStruct(modulate.shape, jnp.float32),
             jax.ShapeDtypeStruct(own_latent.shape, jnp.float32),
             jax.ShapeDtypeStruct(timesteps.shape, jnp.int32),
         ),
-        in_specs=[pl.BlockSpec(memory_space=pl.ANY)] * 7,
+        in_specs=[pl.BlockSpec(memory_space=pl.ANY)] * 6,
         out_specs=(pl.BlockSpec(memory_space=pltpu.VMEM),) * 6,
         scratch_shapes=[
             pltpu.SemaphoreType.DMA((4,)),
-            pltpu.SemaphoreType.DMA((3,)),
+            pltpu.SemaphoreType.DMA((2,)),
         ],
         compiler_params=pltpu.CompilerParams(vmem_limit_bytes=24 * 2**20),
         cost_estimate=pl.CostEstimate(
             flops=2 * half * width * w_in.shape[0], bytes_accessed=6 * width * PAIR, transcendentals=0
         ),
-    )(own_latent, modulate, w_in, timesteps, w_query, w_key, w_value)
-
-
-def attention_kernel(
-    other_latent, own_normed, first, w_in, modulate, w_query, w_key, w_value, w_attn_out,
-    send, own_mixed, w_out_held, normed, mixed, w_held, sems,
-):
+    )(own_latent, modulate, w_in, timesteps, w_query, w_key)
+
+
+def norm_kernel(other_latent, own_normed, w_in, modulate, normed):
     half = other_latent.shape[1]
-    blocks = 1 + w_held.shape[0]
-    queue = []
-    for block in range(1, blocks):
-        for which, weight in enumerate((w_query, w_key, w_value)):
-            queue.append((weight.at[:, pl.ds(block * PAIR, PAIR)], w_held.at[block - 1, which]))
-    for row in range(0, w_attn_out.shape[0], PAIR):
-        rows = pl.ds(row, PAIR)
-        queue.append((w_attn_out.at[rows, :], w_out_held.at[rows, :]))
-    queue = [pltpu.make_async_copy(*ends, sems.at[i]) for i, ends in enumerate(queue)]
-    waited = []
-
-    def arrive():
-        queue[len(waited)].wait()
-        if len(waited) + AHEAD < len(queue):
-            queue[len(waited) + AHEAD].start()
-        waited.append(True)
-
-    for copy in queue[:AHEAD]:
-        copy.start()
-
     normed[:half, :] = own_normed[...]
     normed[half:, :] = shaped(hidden_of(other_latent[...], w_in[...]), 1.0 + modulate[1], modulate[0])
 
-    def project(block, which):
-        weight = first[which] if block == 0 else w_held[block - 1, which]
+
+def norm_all(other_latent, own_normed, w_in, modulate):
+    half, width = own_normed.shape
+    return pl.pallas_call(
+        norm_kernel,
+        out_shape=jax.ShapeDtypeStruct((2 * half, width), jnp.bfloat16),
+        in_specs=[pl.BlockSpec(memory_space=pltpu.VMEM)] * 4,
+        out_specs=pl.BlockSpec(memory_space=pltpu.VMEM),
+        compiler_params=pltpu.CompilerParams(vmem_limit_bytes=24 * 2**20),
+        cost_estimate=pl.CostEstimate(
+            flops=2 * half * width * w_in.shape[0], bytes_accessed=6 * half * width, transcendentals=0
+        ),
+    )(other_latent, own_normed, w_in, modulate)
+
+
+def attention_kernel(
+    normed, first, w_value, w_query, w_key, w_attn_out,
+    send, own_mixed, w_out_held, mixed, w_held, sems,
+):
+    half = normed.shape[0] // 2
+    blocks = 1 + w_held.shape[0]
+    def fetch(block):
+        if block == blocks:
+            return [
+                pltpu.make_async_copy(w_attn_out.at[rows, :], w_out_held.at[rows, :], sems.at[blocks - 1])
+                for place, rows in enumerate(pl.ds(row, PAIR) for row in range(0, w_attn_out.shape[0], PAIR))
+            ]
+        cols = pl.ds(block * PAIR, PAIR)
+        return [
+            pltpu.make_async_copy(weight.at[:, cols], w_held.at[block - 1, which], sems.at[block - 1])
+            for which, weight in enumerate((w_query, w_key))
+        ]
+
+    def arrive(block):
+        held = w_out_held if block == blocks else w_held.at[block - 1]
+        pltpu.make_async_copy(held, held, sems.at[block - 1]).wait()
+
+    def one(block, which):
+        if which == 2:
+            weight = w_value[:, block * PAIR : (block + 1) * PAIR]
+        else:
+            weight = first[which] if block == 0 else w_held[block - 1, which]
         return jnp.dot(normed[...], weight, preferred_element_type=jnp.float32).astype(jnp.bfloat16)
 
+    def project(block):
+        return [one(block, which) for which in range(3)]
+
+    for block in range(1, blocks + 1):
+        for copy in fetch(block):
+            copy.start(priority=int(block > 1))
+
     ones = jnp.ones((2 * half, HEAD_DIM), jnp.bfloat16)
+
+    def score(query, key, head):
+        cols = slice(head * HEAD_DIM, (head + 1) * HEAD_DIM)
+        return lax.dot_general(
+            query[:, cols], key[:, cols], (((1,), (1,)), ((), ())), preferred_element_type=jnp.float32
+        )
+
+    def weigh(scores):
+        peak = jnp.max(scores, axis=-1, keepdims=True)
+        return jnp.exp2((scores - peak) * (HEAD_DIM ** (-0.5) * LOG2_E)).astype(jnp.bfloat16)
+
+    def mix(block, head, weights, value):
+        cols = slice(head * HEAD_DIM, (head + 1) * HEAD_DIM)
+        both = jnp.dot(
+            weights, jnp.concatenate([value[:, cols], ones], axis=1), preferred_element_type=jnp.float32
+        )
+        result = (both[:, :HEAD_DIM] / both[:, HEAD_DIM:]).astype(jnp.bfloat16)
+        col = block * PAIR + head * HEAD_DIM
+        own_mixed[:, col : col + HEAD_DIM] = result[:half]
+        mixed[:, col : col + HEAD_DIM] = result[half:]
 
     def attend(block, query, key, value):
         for head in range(PAIR // HEAD_DIM):
-            cols = slice(head * HEAD_DIM, (head + 1) * HEAD_DIM)
-            scores = lax.dot_general(
-                query[:, cols], key[:, cols], (((1,), (1,)), ((), ())), preferred_element_type=jnp.float32
-            )
-            peak = jnp.max(scores, axis=-1, keepdims=True)
-            weights = jnp.exp2((scores - peak) * (HEAD_DIM ** (-0.5) * LOG2_E)).astype(jnp.bfloat16)
-            both = jnp.dot(
-                weights,
-                jnp.concatenate([value[:, cols], ones], axis=1),
-                preferred_element_type=jnp.float32,
-            )
-            result = (both[:, :HEAD_DIM] / both[:, HEAD_DIM:]).astype(jnp.bfloat16)
-            col = block * PAIR + head * HEAD_DIM
-            own_mixed[:, col : col + HEAD_DIM] = result[:half]
-            mixed[:, col : col + HEAD_DIM] = result[half:]
-
-    before = [project(0, which) for which in range(3)]
+            mix(block, head, weigh(score(query, key, head)), value)
+
+    before = project(0)
     for block in range(1, blocks):
-        for which in range(3):
-            arrive()
-        projected = [project(block, which) for which in range(3)]
+        arrive(block)
+        projected = project(block)
         attend(block - 1, *before)
         before = projected
     attend(blocks - 1, *before)
-    while len(waited) < len(queue):
-        arrive()
+    arrive(blocks)
     for col in range(0, send.shape[1], PAIR):
         cols = slice(col, col + PAIR)
         send[:, cols] = jnp.dot(
@@ -151,8 +180,8 @@
         ).astype(jnp.bfloat16)
 
 
-def attention(other_latent, own_normed, first, w_in, modulate, w_query, w_key, w_value, w_attn_out):
-    half = other_latent.shape[1]
+def attention(normed, first, w_value, w_query, w_key, w_attn_out):
+    half = normed.shape[0] // 2
     width, cols = w_query.shape
     blocks = cols // PAIR
     return pl.pallas_call(
@@ -162,19 +191,18 @@
             jax.ShapeDtypeStruct((half, cols), jnp.bfloat16),
             jax.ShapeDtypeStruct(w_attn_out.shape, jnp.bfloat16),
         ),
-        in_specs=[pl.BlockSpec(memory_space=pltpu.VMEM)] * 5 + [pl.BlockSpec(memory_space=pl.ANY)] * 4,
+        in_specs=[pl.BlockSpec(memory_space=pltpu.VMEM)] * 3 + [pl.BlockSpec(memory_space=pl.ANY)] * 3,
         out_specs=(pl.BlockSpec(memory_space=pltpu.VMEM),) * 3,
         scratch_shapes=[
-            pltpu.VMEM((2 * half, width), jnp.bfloat16),
             pltpu.VMEM((half, cols), jnp.bfloat16),
-            pltpu.VMEM((blocks - 1, 3, width, PAIR), jnp.bfloat16),
-            pltpu.SemaphoreType.DMA((4 * blocks - 3,)),
+            pltpu.VMEM((blocks - 1, 2, width, PAIR), jnp.bfloat16),
+            pltpu.SemaphoreType.DMA((blocks,)),
         ],
         compiler_params=pltpu.CompilerParams(vmem_limit_bytes=32 * 2**20),
         cost_estimate=pl.CostEstimate(
             flops=2 * 2 * half * width * cols * 4, bytes_accessed=2 * width * cols * 4, transcendentals=0
         ),
-    )(other_latent, own_normed, first, w_in, modulate, w_query, w_key, w_value, w_attn_out)
+    )(normed, first, w_value, w_query, w_key, w_attn_out)
 
 
 def own_rows_kernel(own_latent, w_in, modulate, timesteps, chosen, own_mixed, w_attn_out, out, step_size):
@@ -252,12 +280,11 @@
     modulate = jnp.transpose(modulation, (1, 0, 2))
     there = [
         pltpu.with_memory_space_constraint(array, pltpu.HBM)
-        for array in (own_latent, modulate, w_in, timesteps[None], w_query, w_key, w_value, w_attn_out)
+        for array in (own_latent, modulate, w_in, timesteps[None], w_query, w_key, w_attn_out)
     ]
-    own_normed, first, w_in_held, modulate, own_latent, times = front(*there[:7])
-    send, own_mixed, w_out_held = attention(
-        other_latent, own_normed, first, w_in_held, modulate, *there[4:]
-    )
+    own_normed, first, w_in_held, modulate, own_latent, times = front(*there[:6])
+    normed = norm_all(other_latent, own_normed, w_in_held, modulate)
+    send, own_mixed, w_out_held = attention(normed, first, w_value, *there[4:])
     received = lax.ppermute(send, "seq", swap)
     ahead = jnp.arange(timesteps.shape[0], dtype=jnp.int32)[None] - lax.axis_index("tm")
     chosen = (ahead == jnp.arange(2, dtype=jnp.int32)[:, None]).astype(jnp.float32)

time: 60.7 us -> 60.1 us (level)
  Pallas kernels: 11 us -> 10.1 us
    pallas_call x1, Pallas kernels: 7.89 us -> 6.61 us  [attention(): pl.pallas_call(attention_kernel, out_shape=(jax.ShapeDtypeStruct((half, w...]
    pallas_call x0 -> x1, Pallas kernels: none -> 0.68 us  [norm_all(): pl.pallas_call(norm_kernel, out_shape=jax.ShapeDtypeStruct((2 * half, wid...]
where the time goes in v5:
time: 60.1 us; the launch traced here: 59.9 us
  blocking collectives  35.3 us (59%)
  starting transfers between devices  10.8 us (18%)
  Pallas kernels  10.1 us (17%)
  other arithmetic  1.35 us (2%)
  waiting for transfers between devices  0.92 us (2%)
  matrix products  0.72 us (1%)
    all_to_all x1, blocking collectives, prefix_over_steps(): lax.all_to_all(sums, 'tm', 0, 0, axis_index_groups=same(count, lambda x,...  24.6 us
    all_to_all x1, blocking collectives, prefix_over_steps(): lax.all_to_all(block, 'tm', 0, 0, axis_index_groups=same(count, lambda x,...  10.7 us
    ppermute x1, starting transfers between devices, on_device(): other_latent = lax.ppermute(own_latent, 'seq', swap)  8.91 us
    pallas_call x1, Pallas kernels, attention(): pl.pallas_call(attention_kernel, out_shape=(jax.ShapeDtypeStruct((half, w...  6.61 us
    ppermute x1, starting transfers between devices, on_device(): received = lax.ppermute(send, 'seq', swap)  1.92 us
    pallas_call x1, Pallas kernels, front(): pl.pallas_call(front_kernel, out_shape=(jax.ShapeDtypeStruct((half, width...  1.9 us
  transfers between devices with their start and end apart: 2, of which 1 were waited for; matrix products, arithmetic and copies ran while one was open for 0% of the time, Pallas kernels for 5%

profile of v5, /device:TPU:1, one launch (start us, length us, event | category | flops | bytes accessed | tf_op | source)
XLA Modules:
  0.0 59.9 jit_solution(14437509741172758377)
XLA Ops:
  0.0 0.0 copy-start
  0.0 8.9 %collective-permute-start = (f32[64,128]{1,0:T(8,128)}, f32[64,128]{1,0:T(8,128)S(1)}, u32[]{:S(2)}, u32[]{:S(2)}) collective-permute-start(f32[64,128]{1,0:T(8,128)} %bitcast.23), channel_id=1, source_target_pairs={{0,1},{1,0},{2,3},{3,2},{4,5},{5,4},{6,7},{7,6},{8,9},{9,8},{10,11... | collective-permute-start | bytes 98312 | tf_op jit(solution)/shard_map/ppermute | solution.py:279
  9.0 0.1 compare_convert_fusion
  9.1 0.0 copy-start.1
  9.1 1.9 %shard_map.91 = (bf16[128,2048]{1,0:T(8,128)(2,1)S(1)}, bf16[2,2048,256]{2,1,0:T(8,128)(2,1)S(1)}, bf16[64,2048]{1,0:T(8,128)(2,1)S(1)}, f32[5,1,2048]{2,1,0:T(1...) custom-call(f32[64,128]{1,0:T(8,128)} %bitcast.24, f32[5,1,2048]{2,1,0:T(1,128)} %bitcast.22, ...), custom_call_target="tpu_custom_call" | custom-call | flops 33554432 | bytes 3145728 | tf_op jit(solution)/shard_map/pallas_call | solution.py:63
  11.0 0.0 collective-permute-done.other_latent
  11.0 0.7 %shard_map.92.normed = bf16[256,2048]{1,0:T(8,128)(2,1)S(1)} custom-call(f32[64,128]{1,0:T(8,128)S(1)} %collective-permute-done.other_latent, bf16[128,2048]{1,0:T(8,128)(2,1)S(1)} %get-tuple-element.22.own_normed, bf16[64,2048]{1,0:T(8,128)(2,1)S(1)} %get-tuple-element.19.w_in, f32[5,1,2048]{2,1,0:T(1,128)S(1)} %get-tuple-element.20.modulate), custom_call_target="tpu_custom_call" | custom-call | flops 33554432 | bytes 1572864 | tf_op jit(solution)/shard_map/pallas_call | solution.py:94
  11.7 0.4 copy-done.1
  12.1 6.6 %shard_map.93 = (bf16[128,2048]{1,0:T(8,128)(2,1)S(1)}, bf16[128,1024]{1,0:T(8,128)(2,1)S(1)}, bf16[1024,2048]{1,0:T(8,128)(2,1)S(1)}) custom-call(bf16[256,2048]{1,0:T(8,128)(2,1)S(1)} %shard_map.92.normed, bf16[2,2048,256]{2,1,0:T(8,128)(2,1)S(1)} %get-tuple-element.23.first, bf16[2048,1024]{1,0:T(8,128)(2,1)S(1)} %copy-done.1, ...), custom_call_target="tpu_custom_call" | custom-call | flops 4294967296 | bytes 16777216 | tf_op jit(solution)/shard_map/pallas_call | solution.py:187
  18.7 1.9 %collective-permute-start.1 = (bf16[128,2048]{1,0:T(8,128)(2,1)S(1)}, bf16[128,2048]{1,0:T(8,128)(2,1)S(1)}, u32[]{:S(2)}, u32[]{:S(2)}) collective-permute-start(bf16[128,2048]{1,0:T(8,128)(2,1)S(1)} %get-tuple-element.28), channel_id=1, source_target_pairs={{0,1},{1,0},{2,3},{3,2},{4,5},{5,4},{6,7},{7,6},{8,9},{9,8},{10,11... | collective-permute-start | bytes 1572872 | tf_op jit(solution)/shard_map/ppermute | solution.py:288
  20.7 0.9 %shard_map.94 = (f32[128,2048]{1,0:T(8,128)S(1)}, f32[1,128]{1,0:T(1,128)S(1)}) custom-call(f32[64,128]{1,0:T(8,128)S(1)} %get-tuple-element.18.own_latent, bf16[64,2048]{1,0:T(8,128)(2,1)S(1)} %get-tuple-element.19.w_in, f32[5,1,2048]{2,1,0:T(1,128)S(1)} %get-tuple-element.20.modulate, s32[1,256]{1,0:T(1,128)S(1)} %get-tuple-element.21.timesteps, ...), custom_call_target="tpu_custom_call" | custom-call | flops 536870912 | bytes 1048576 | tf_op jit(solution)/shard_map/pallas_call | solution.py:224
  21.6 0.9 %collective-permute-done.1 = bf16[128,2048]{1,0:T(8,128)(2,1)S(1)} collective-permute-done((bf16[128,2048]{1,0:T(8,128)(2,1)S(1)}, bf16[128,2048]{1,0:T(8,128)(2,1)S(1)}, u32[]{:S(2)}, u32[]{:S(2)}) %collective-permute-start.1) | collective-permute-done | bytes 524320 | tf_op jit(solution)/shard_map/ppermute | solution.py:288
  22.5 0.2 fusion.6
  22.8 0.3 multiply_reduce_fusion
  23.1 0.0 copy-done
  23.1 0.5 fusion.1
  23.6 10.7 %all_to_all.10 = bf16[16,64,128]{2,1,0:T(8,128)(2,1)S(1)} all-to-all(bf16[16,64,128]{2,1,0:T(8,128)(2,1)S(1)} %broadcast_in_dim.7), channel_id=1, replica_groups={{0,2,4,6,8,10,12,14,64,66,68,70,72,74,76,78},{16,18,20,22,24,26,28,30,8..., dimensions={0} | all-to-all | bytes 524288 | tf_op jit(solution)/shard_map/all_to_all | solution.py:264
  34.3 0.3 convolution_convert_fusion
  34.6 0.1 copy.11
  34.6 24.6 %all_to_all.11 = bf16[16,64,128]{2,1,0:T(8,128)(2,1)S(1)} all-to-all(bf16[16,64,128]{2,1,0:T(8,128)(2,1)S(1)} %copy.11), channel_id=1, replica_groups={{0,16,32,48,128,144,160,176,256,272,288,304,384,400,416,432},{2,18,34,5..., dimensions={0} | all-to-all | bytes 524288 | tf_op jit(solution)/shard_map/all_to_all | solution.py:270
  59.3 0.7 %convert_reduce_fusion = f32[64,128]{1,0:T(8,128)} fusion(bf16[16,64,128]{2,1,0:T(8,128)(2,1)S(1)} %all_to_all.11), kind=kLoop, calls=%fused_computation.7 | loop fusion | flops 253952 | bytes 294912 | tf_op jit(solution)/shard_map/reduce_sum | solution.py:273
  (7 shorter events, 0.1 us)
Async XLA Ops:
  0.0 23.1 %copy-start = (bf16[2048,64]{0,1:T(8,128)(2,1)S(1)}, bf16[2048,64]{0,1:T(8,128)(2,1)}, u32[]{:S(2)}) copy-start(bf16[2048,64]{0,1:T(8,128)(2,1)} %param.17) | copy-start | bytes 786436
  0.0 11.0 %collective-permute-start = (f32[64,128]{1,0:T(8,128)}, f32[64,128]{1,0:T(8,128)S(1)}, u32[]{:S(2)}, u32[]{:S(2)}) collective-permute-start(f32[64,128]{1,0:T(8,128)} %bitcast.23), channel_id=1, source_target_pairs={{0,1},{1,0},{2,3},{3,2},{4,5},{5,4},{6,7},{7,6},{8,9},{9,8},{10,11... | collective-permute-start | bytes 98312 | tf_op jit(solution)/shard_map/ppermute | solution.py:279
  9.1 3.0 %copy-start.1 = (bf16[2048,1024]{1,0:T(8,128)(2,1)S(1)}, bf16[2048,1024]{1,0:T(8,128)(2,1)}, u32[]{:S(2)}) copy-start(bf16[2048,1024]{1,0:T(8,128)(2,1)} %w_value.1) | copy-start | bytes 12582916
  18.7 3.8 %collective-permute-start.1 = (bf16[128,2048]{1,0:T(8,128)(2,1)S(1)}, bf16[128,2048]{1,0:T(8,128)(2,1)S(1)}, u32[]{:S(2)}, u32[]{:S(2)}) collective-permute-start(bf16[128,2048]{1,0:T(8,128)(2,1)S(1)} %get-tuple-element.28), channel_id=1, source_target_pairs={{0,1},{1,0},{2,3},{3,2},{4,5},{5,4},{6,7},{7,6},{8,9},{9,8},{10,11... | collective-permute-start | bytes 1572872 | tf_op jit(solution)/shard_map/ppermute | solution.py:288

commit v6 on v5

--- a/solution.py
+++ b/solution.py
@@ -103,9 +103,23 @@
     )(other_latent, own_normed, w_in, modulate)
 
 
+def attend_head(query, key, value, head):
+    cols = slice(head * HEAD_DIM, (head + 1) * HEAD_DIM)
+    scores = lax.dot_general(
+        query[:, cols], key[:, cols], (((1,), (1,)), ((), ())), preferred_element_type=jnp.float32
+    )
+    peak = jnp.max(scores, axis=-1, keepdims=True)
+    weights = jnp.exp2((scores - peak) * (HEAD_DIM ** (-0.5) * LOG2_E)).astype(jnp.bfloat16)
+    ones = jnp.ones((value.shape[0], HEAD_DIM), jnp.bfloat16)
+    both = jnp.dot(
+        weights, jnp.concatenate([value[:, cols], ones], axis=1), preferred_element_type=jnp.float32
+    )
+    return (both[:, :HEAD_DIM] / both[:, HEAD_DIM:]).astype(jnp.bfloat16)
+
+
 def attention_kernel(
     normed, first, w_value, w_query, w_key, w_attn_out,
-    send, own_mixed, w_out_held, mixed, w_held, sems,
+    send, own_mixed, w_out_held, last_query, last_key, last_value, mixed, w_held, sems,
 ):
     half = normed.shape[0] // 2
     blocks = 1 + w_held.shape[0]
@@ -171,7 +185,11 @@
         projected = project(block)
         attend(block - 1, *before)
         before = projected
-    attend(blocks - 1, *before)
+    query, key, value = before
+    last_query[...], last_key[...], last_value[...] = query[:half], key, value
+    for head in range(PAIR // HEAD_DIM):
+        col = (blocks - 1) * PAIR + head * HEAD_DIM
+        mixed[:, col : col + HEAD_DIM] = attend_head(query[half:], key, value, head)
     arrive(blocks)
     for col in range(0, send.shape[1], PAIR):
         cols = slice(col, col + PAIR)
@@ -190,9 +208,12 @@
             jax.ShapeDtypeStruct((half, width), jnp.bfloat16),
             jax.ShapeDtypeStruct((half, cols), jnp.bfloat16),
             jax.ShapeDtypeStruct(w_attn_out.shape, jnp.bfloat16),
+            jax.ShapeDtypeStruct((half, PAIR), jnp.bfloat16),
+            jax.ShapeDtypeStruct((2 * half, PAIR), jnp.bfloat16),
+            jax.ShapeDtypeStruct((2 * half, PAIR), jnp.bfloat16),
         ),
         in_specs=[pl.BlockSpec(memory_space=pltpu.VMEM)] * 3 + [pl.BlockSpec(memory_space=pl.ANY)] * 3,
-        out_specs=(pl.BlockSpec(memory_space=pltpu.VMEM),) * 3,
+        out_specs=(pl.BlockSpec(memory_space=pltpu.VMEM),) * 6,
         scratch_shapes=[
             pltpu.VMEM((half, cols), jnp.bfloat16),
             pltpu.VMEM((blocks - 1, 2, width, PAIR), jnp.bfloat16),
@@ -205,20 +226,25 @@
     )(normed, first, w_value, w_query, w_key, w_attn_out)
 
 
-def own_rows_kernel(own_latent, w_in, modulate, timesteps, chosen, own_mixed, w_attn_out, out, step_size):
+def own_rows_kernel(own_latent, w_in, modulate, timesteps, chosen, own_mixed, w_attn_out, query, key, value, out, step_size, mixed):
+    last = own_mixed.shape[1] - PAIR
+    mixed[:, :last] = own_mixed[:, :last]
+    for head in range(PAIR // HEAD_DIM):
+        col = last + head * HEAD_DIM
+        mixed[:, col : col + HEAD_DIM] = attend_head(query[...], key[...], value[...], head)
     times = jnp.sum(timesteps[...].astype(jnp.float32) * chosen[...], axis=1, keepdims=True)
     step_size[...] = jnp.broadcast_to((times[1:] - times[:1]) / TSCALE, step_size.shape)
     for col in range(0, out.shape[1], PAIR):
         cols = slice(col, col + PAIR)
         partial = jnp.dot(
-            own_mixed[...], w_attn_out[:, cols], preferred_element_type=jnp.float32
+            mixed[...], w_attn_out[:, cols], preferred_element_type=jnp.float32
         ).astype(jnp.bfloat16)
         out[:, cols] = hidden_of(own_latent[...], w_in[:, cols]) + modulate[2, :, cols] * partial.astype(
             jnp.float32
         )
 
 
-def own_rows(own_latent, w_in, modulate, timesteps, chosen, own_mixed, w_attn_out):
+def own_rows(own_latent, w_in, modulate, timesteps, chosen, own_mixed, w_attn_out, *last):
     half, cols = own_mixed.shape
     width = w_attn_out.shape[1]
     return pl.pallas_call(
@@ -227,13 +253,14 @@
             jax.ShapeDtypeStruct((half, width), jnp.float32),
             jax.ShapeDtypeStruct((1, half), jnp.float32),
         ),
-        in_specs=[pl.BlockSpec(memory_space=pltpu.VMEM)] * 7,
+        in_specs=[pl.BlockSpec(memory_space=pltpu.VMEM)] * 10,
         out_specs=(pl.BlockSpec(memory_space=pltpu.VMEM),) * 2,
+        scratch_shapes=[pltpu.VMEM(own_mixed.shape, jnp.bfloat16)],
         compiler_params=pltpu.CompilerParams(vmem_limit_bytes=24 * 2**20),
         cost_estimate=pl.CostEstimate(
             flops=2 * half * width * cols, bytes_accessed=4 * half * width, transcendentals=0
         ),
-    )(own_latent, w_in, modulate, timesteps, chosen, own_mixed, w_attn_out)
+    )(own_latent, w_in, modulate, timesteps, chosen, own_mixed, w_attn_out, *last)
 
 
 def same(count, key):
@@ -284,12 +311,12 @@
     ]
     own_normed, first, w_in_held, modulate, own_latent, times = front(*there[:6])
     normed = norm_all(other_latent, own_normed, w_in_held, modulate)
-    send, own_mixed, w_out_held = attention(normed, first, w_value, *there[4:])
+    send, own_mixed, w_out_held, *last = attention(normed, first, w_value, *there[4:])
     received = lax.ppermute(send, "seq", swap)
     ahead = jnp.arange(timesteps.shape[0], dtype=jnp.int32)[None] - lax.axis_index("tm")
     chosen = (ahead == jnp.arange(2, dtype=jnp.int32)[:, None]).astype(jnp.float32)
     own_part, step_size = own_rows(
-        own_latent, w_in_held, modulate, times, chosen, own_mixed, w_out_held
+        own_latent, w_in_held, modulate, times, chosen, own_mixed, w_out_held, *last
     )
     resid = own_part + modulate[2] * received.astype(jnp.float32)
     final = (layer_norm(resid) * (1.0 + modulate[4]) + modulate[3]).astype(jnp.bfloat16)

time: 60.1 us -> 60.5 us (level)
  Pallas kernels: 10.1 us -> 10.8 us
where the time goes in v6:
time: 60.5 us; the launch traced here: 60.3 us
  blocking collectives  35.3 us (58%)
  starting transfers between devices  10.8 us (18%)
  Pallas kernels  10.8 us (18%)
  other arithmetic  1.35 us (2%)
  matrix products  0.72 us (1%)
  waiting for transfers between devices  0.67 us (1%)
    all_to_all x1, blocking collectives, prefix_over_steps(): lax.all_to_all(sums, 'tm', 0, 0, axis_index_groups=same(count, lambda x,...  24.6 us
    all_to_all x1, blocking collectives, prefix_over_steps(): lax.all_to_all(block, 'tm', 0, 0, axis_index_groups=same(count, lambda x,...  10.7 us
    ppermute x1, starting transfers between devices, on_device(): other_latent = lax.ppermute(own_latent, 'seq', swap)  8.91 us
    pallas_call x1, Pallas kernels, attention(): pl.pallas_call(attention_kernel, out_shape=(jax.ShapeDtypeStruct((half, w...  7.03 us
    ppermute x1, starting transfers between devices, on_device(): received = lax.ppermute(send, 'seq', swap)  1.93 us
    pallas_call x1, Pallas kernels, front(): pl.pallas_call(front_kernel, out_shape=(jax.ShapeDtypeStruct((half, width...  1.9 us
  transfers between devices with their start and end apart: 2, of which 1 were waited for; matrix products, arithmetic and copies ran while one was open for 0% of the time, Pallas kernels for 5%

profile of v6, /device:TPU:1, one launch (start us, length us, event | category | flops | bytes accessed | tf_op | source)
XLA Modules:
  0.0 60.3 jit_solution(6845535268201305665)
XLA Ops:
  0.0 0.0 copy-start
  0.0 8.9 %collective-permute-start = (f32[64,128]{1,0:T(8,128)}, f32[64,128]{1,0:T(8,128)S(1)}, u32[]{:S(2)}, u32[]{:S(2)}) collective-permute-start(f32[64,128]{1,0:T(8,128)} %bitcast.23), channel_id=1, source_target_pairs={{0,1},{1,0},{2,3},{3,2},{4,5},{5,4},{6,7},{7,6},{8,9},{9,8},{10,11... | collective-permute-start | bytes 98312 | tf_op jit(solution)/shard_map/ppermute | solution.py:306
  9.0 0.1 compare_convert_fusion
  9.1 0.0 copy-start.1
  9.1 1.9 %shard_map.91 = (bf16[128,2048]{1,0:T(8,128)(2,1)S(1)}, bf16[2,2048,256]{2,1,0:T(8,128)(2,1)S(1)}, bf16[64,2048]{1,0:T(8,128)(2,1)S(1)}, f32[5,1,2048]{2,1,0:T(1...) custom-call(f32[64,128]{1,0:T(8,128)} %bitcast.24, f32[5,1,2048]{2,1,0:T(1,128)} %bitcast.22, ...), custom_call_target="tpu_custom_call" | custom-call | flops 33554432 | bytes 3145728 | tf_op jit(solution)/shard_map/pallas_call | solution.py:63
  11.0 0.0 collective-permute-done.other_latent
  11.0 0.7 %shard_map.92.normed = bf16[256,2048]{1,0:T(8,128)(2,1)S(1)} custom-call(f32[64,128]{1,0:T(8,128)S(1)} %collective-permute-done.other_latent, bf16[128,2048]{1,0:T(8,128)(2,1)S(1)} %get-tuple-element.25.own_normed, bf16[64,2048]{1,0:T(8,128)(2,1)S(1)} %get-tuple-element.22.w_in, f32[5,1,2048]{2,1,0:T(1,128)S(1)} %get-tuple-element.23.modulate), custom_call_target="tpu_custom_call" | custom-call | flops 33554432 | bytes 1572864 | tf_op jit(solution)/shard_map/pallas_call | solution.py:94
  11.7 0.4 copy-done.1
  12.1 7.0 %shard_map.93 = (bf16[128,2048]{1,0:T(8,128)(2,1)S(1)}, bf16[128,1024]{1,0:T(8,128)(2,1)S(1)}, bf16[1024,2048]{1,0:T(8,128)(2,1)S(1)}, bf16[128,256]{1,0:T(8,128...) custom-call(bf16[256,2048]{1,0:T(8,128)(2,1)S(1)} %shard_map.92.normed, ...), custom_call_target="tpu_custom_call" | custom-call | flops 4294967296 | bytes 16777216 | tf_op jit(solution)/shard_map/pallas_call | solution.py:205
  19.1 1.9 %collective-permute-start.1 = (bf16[128,2048]{1,0:T(8,128)(2,1)S(1)}, bf16[128,2048]{1,0:T(8,128)(2,1)S(1)}, u32[]{:S(2)}, u32[]{:S(2)}) collective-permute-start(bf16[128,2048]{1,0:T(8,128)(2,1)S(1)} %get-tuple-element.34), channel_id=1, source_target_pairs={{0,1},{1,0},{2,3},{3,2},{4,5},{5,4},{6,7},{7,6},{8,9},{9,8},{10,11... | collective-permute-start | bytes 1572872 | tf_op jit(solution)/shard_map/ppermute | solution.py:315
  21.1 1.2 %shard_map.94 = (f32[128,2048]{1,0:T(8,128)S(1)}, f32[1,128]{1,0:T(1,128)S(1)}) custom-call(f32[64,128]{1,0:T(8,128)S(1)} %get-tuple-element.21.own_latent, bf16[64,2048]{1,0:T(8,128)(2,1)S(1)} %get-tuple-element.22.w_in, f32[5,1,2048]{2,1,0:T(1,128)S(1)} %get-tuple-element.23.modulate, s32[1,256]{1,0:T(1,128)S(1)} %get-tuple-element.24.timesteps, ...), custom_call_target="tpu_custom_call" | custom-call | flops 536870912 | bytes 1048576 | tf_op jit(solution)/shard_map/pallas_call | solution.py:250
  22.3 0.7 %collective-permute-done.1 = bf16[128,2048]{1,0:T(8,128)(2,1)S(1)} collective-permute-done((bf16[128,2048]{1,0:T(8,128)(2,1)S(1)}, bf16[128,2048]{1,0:T(8,128)(2,1)S(1)}, u32[]{:S(2)}, u32[]{:S(2)}) %collective-permute-start.1) | collective-permute-done | bytes 524320 | tf_op jit(solution)/shard_map/ppermute | solution.py:315
  22.9 0.2 fusion.6
  23.2 0.3 multiply_reduce_fusion
  23.5 0.0 copy-done
  23.5 0.5 fusion.1
  24.1 10.7 %all_to_all.10 = bf16[16,64,128]{2,1,0:T(8,128)(2,1)S(1)} all-to-all(bf16[16,64,128]{2,1,0:T(8,128)(2,1)S(1)} %broadcast_in_dim.7), channel_id=1, replica_groups={{0,2,4,6,8,10,12,14,64,66,68,70,72,74,76,78},{16,18,20,22,24,26,28,30,8..., dimensions={0} | all-to-all | bytes 524288 | tf_op jit(solution)/shard_map/all_to_all | solution.py:291
  34.7 0.3 convolution_convert_fusion
  35.0 0.1 copy.11
  35.1 24.6 %all_to_all.11 = bf16[16,64,128]{2,1,0:T(8,128)(2,1)S(1)} all-to-all(bf16[16,64,128]{2,1,0:T(8,128)(2,1)S(1)} %copy.11), channel_id=1, replica_groups={{0,16,32,48,128,144,160,176,256,272,288,304,384,400,416,432},{2,18,34,5..., dimensions={0} | all-to-all | bytes 524288 | tf_op jit(solution)/shard_map/all_to_all | solution.py:297
  59.7 0.7 %convert_reduce_fusion = f32[64,128]{1,0:T(8,128)} fusion(bf16[16,64,128]{2,1,0:T(8,128)(2,1)S(1)} %all_to_all.11), kind=kLoop, calls=%fused_computation.7 | loop fusion | flops 253952 | bytes 294912 | tf_op jit(solution)/shard_map/reduce_sum | solution.py:300
  (7 shorter events, 0.1 us)
Async XLA Ops:
  0.0 23.5 %copy-start = (bf16[2048,64]{0,1:T(8,128)(2,1)S(1)}, bf16[2048,64]{0,1:T(8,128)(2,1)}, u32[]{:S(2)}) copy-start(bf16[2048,64]{0,1:T(8,128)(2,1)} %param.17) | copy-start | bytes 786436
  0.0 11.0 %collective-permute-start = (f32[64,128]{1,0:T(8,128)}, f32[64,128]{1,0:T(8,128)S(1)}, u32[]{:S(2)}, u32[]{:S(2)}) collective-permute-start(f32[64,128]{1,0:T(8,128)} %bitcast.23), channel_id=1, source_target_pairs={{0,1},{1,0},{2,3},{3,2},{4,5},{5,4},{6,7},{7,6},{8,9},{9,8},{10,11... | collective-permute-start | bytes 98312 | tf_op jit(solution)/shard_map/ppermute | solution.py:306
  9.1 3.0 %copy-start.1 = (bf16[2048,1024]{1,0:T(8,128)(2,1)S(1)}, bf16[2048,1024]{1,0:T(8,128)(2,1)}, u32[]{:S(2)}) copy-start(bf16[2048,1024]{1,0:T(8,128)(2,1)} %w_value.1) | copy-start | bytes 12582916
  19.1 3.8 %collective-permute-start.1 = (bf16[128,2048]{1,0:T(8,128)(2,1)S(1)}, bf16[128,2048]{1,0:T(8,128)(2,1)S(1)}, u32[]{:S(2)}, u32[]{:S(2)}) collective-permute-start(bf16[128,2048]{1,0:T(8,128)(2,1)S(1)} %get-tuple-element.34), channel_id=1, source_target_pairs={{0,1},{1,0},{2,3},{3,2},{4,5},{5,4},{6,7},{7,6},{8,9},{9,8},{10,11... | collective-permute-start | bytes 1572872 | tf_op jit(solution)/shard_map/ppermute | solution.py:315
